TPU v7x, 128 devices: a whole 4x4x4 slice. The times are simulated.
128 devices in a mesh: replica: 4 (over x), fsdp: 32 (over z, y, core).
Axes of the slice: x: 4, y: 4, z: 4, core: 2. Of those that a mesh axis runs over, the one named last changes fastest.
Arguments:
- gradients: bfloat16 [4, 8192, 8192], P('replica', 'fsdp'), may hold values from -0.3984375 to 0.3984375
- projection: bfloat16 [8192, 512], P('fsdp'), may hold values from -0.25 to 0.25
- plan: int32 [256], replicated, may hold values from 0 to 255, each once
- first_codes: bfloat16 [8192, 512], P(('replica', 'fsdp')), may hold values from -1 to 1
- first_scales: float32 [8192, 2], P(('replica', 'fsdp')), may hold values from 0.02 to 0.08
- second_codes: bfloat16 [8192, 512], P(('replica', 'fsdp')), may hold values from 0.099609375 to 1
- second_scales: float32 [8192, 2], P(('replica', 'fsdp')), may hold values from 0.0001 to 0.0004
Outputs:
- update: bfloat16 [8192, 8192], P('fsdp')
- new_first_codes: bfloat16 [8192, 512], P(('replica', 'fsdp'))
- new_first_scales: float32 [8192, 2], P(('replica', 'fsdp'))
- new_second_codes: bfloat16 [8192, 512], P(('replica', 'fsdp'))
- new_second_scales: float32 [8192, 2], P(('replica', 'fsdp'))
Inputs may be any that keep to these rules, and one draw needn't show every extreme that they name: `plan`: each of the 256 panels appears once.
All inputs are finite; a program needn't handle non-finite values. Where the computation divides by a largest or mean magnitude, that divisor is 1e-20 or more.
Results may differ from a plain program's by a relative error of at most 0.014.
Values may be sent and summed in bfloat16 or wider, within the bound.
A program may use at most 64 MiB of HBM per device.

v0:
```python
import jax
import jax.numpy as jnp
from jax import lax
from jax.sharding import PartitionSpec as P

PW = 32
QB = 256
STEP = 2


beta_one = 0.9
beta_two = 0.999
adam_eps = 1e-08
scale_eps = 1e-06


def expand(code_vals, scales):
    blocks = code_vals.astype(jnp.float32).reshape(code_vals.shape[0], -1, QB)
    return (blocks * scales[:, :, None]).reshape(code_vals.shape)


def requant(values):
    blocks = values.reshape(values.shape[0], -1, QB)
    peak = jnp.max(jnp.abs(blocks), axis=2) + scale_eps
    return ((blocks / peak[:, :, None]).reshape(values.shape).astype(jnp.bfloat16), peak)


def local(gradients, projection, plan, first_codes, first_scales, second_codes, second_scales):
    row_count = gradients.shape[1]
    col_count = gradients.shape[2]
    panel_count = col_count // PW
    grad_local = gradients[0].reshape(row_count, panel_count, PW)
    reordered = jnp.take(grad_local, plan, axis=1).reshape(row_count, col_count)
    summed = lax.psum_scatter(reordered, "replica", scatter_dimension=1, tiled=True).astype(
        jnp.float32
    )
    columns = lax.all_to_all(
        summed.astype(jnp.bfloat16), "fsdp", split_axis=1, concat_axis=0, tiled=True
    ).astype(summed.dtype)
    proj_whole = lax.all_gather(projection, "fsdp", axis=0, tiled=True)
    lowrank = lax.dot_general(
        columns,
        proj_whole.astype(jnp.float32),
        (((0,), (0,)), ((), ())),
        precision=lax.Precision.HIGHEST,
    )
    first = expand(first_codes, first_scales)
    second = expand(second_codes, second_scales)
    first_new = beta_one * first + (1.0 - beta_one) * lowrank
    second_new = beta_two * second + (1.0 - beta_two) * lowrank * lowrank
    corr_one = 1.0 - beta_one**STEP
    corr_two = 1.0 - beta_two**STEP
    direction = (first_new / corr_one / (jnp.sqrt(second_new / corr_two) + adam_eps)).astype(
        jnp.bfloat16
    )
    first_out, first_peak = requant(first_new)
    second_out, second_peak = requant(second_new)
    owner_block = lax.dot_general(
        proj_whole, direction, (((1,), (1,)), ((), ())), preferred_element_type=jnp.float32
    ).astype(jnp.bfloat16)
    returned = lax.all_to_all(owner_block, "fsdp", split_axis=0, concat_axis=1, tiled=True)
    ordered = lax.all_gather(returned, "replica", axis=1, tiled=True)
    inverse = (
        jnp.zeros((panel_count,), jnp.int32).at[plan].set(jnp.arange(panel_count, dtype=jnp.int32))
    )
    update = jnp.take(ordered.reshape(row_count, panel_count, PW), inverse, axis=1).reshape(
        row_count, col_count
    )
    return (update, first_out, first_peak, second_out, second_peak)


def solution(mesh):
    in_specs = (
        P("replica", "fsdp", None),
        P("fsdp", None),
        P(),
        P(("replica", "fsdp"), None),
        P(("replica", "fsdp"), None),
        P(("replica", "fsdp"), None),
        P(("replica", "fsdp"), None),
    )
    out_specs = (
        P("fsdp", None),
        P(("replica", "fsdp"), None),
        P(("replica", "fsdp"), None),
        P(("replica", "fsdp"), None),
        P(("replica", "fsdp"), None),
    )
    return jax.shard_map(local, mesh=mesh, in_specs=in_specs, out_specs=out_specs, check_vma=False)
```

profile of v0, /device:TPU:1, one launch (start us, length us, event | category | flops | bytes accessed | tf_op | source)
XLA Modules:
  0.0 196.4 jit_solution(5105665342186875951)
XLA Ops:
  8.0 0.7 compare_select_fusion.1
  8.7 0.7 compare_and_fusion.1
  9.4 6.4 %copy.25 = bf16[1,256,8192]{1,2,0:T(8,128)(2,1)} copy(bf16[1,256,8192]{2,1,0:T(8,128)(2,1)} %param.9) | data formatting | bytes 8388608 | tf_op args[0]
  15.8 4.9 %gather_fusion = bf16[256,256,32]{1,2,0:T(8,128)(2,1)} fusion(bf16[256,256,32]{0,2,1:T(8,128)(2,1)} %bitcast.31, s32[1024]{0:T(1024)S(1)} %pad_clamp_fusion.1), kind=kCustom, calls=%fused_computation.clone | custom fusion | bytes 8389632 | tf_op jit(solution)/shard_map/jit(_take)/gather | solution.py:33
  20.7 4.1 %broadcast_select_fusion.1 = bf16[256,256,32]{1,2,0:T(8,128)(2,1)} fusion(bf16[256,256,32]{1,2,0:T(8,128)(2,1)} %gather_fusion, pred[256]{0:T(512)(128)(4,1)S(1)} %compare_and_fusion.1), kind=kLoop, calls=%fused_computation.5 | loop fusion | flops 2097152 | bytes 8388864 | tf_op jit(solution)/shard_map/jit(_take)/select_n | solution.py:33
  24.9 0.5 all-gather.3.cloned.1.call-update
  25.4 49.6 %reduce-scatter.2.cloned.1.call-done = bf16[256,2048]{0,1:T(8,128)(2,1)} async-done(((bf16[256,8192]{0,1:T(8,128)(2,1)}), bf16[256,2048]{0,1:T(8,128)(2,1)}) %reduce-scatter.2.cloned.1.call-update) | async-done | bytes 1048592 | tf_op jit(solution)/shard_map/reduce_scatter | solution.py:34
  75.0 7.6 %all-to-all-start = ((bf16[256,32,64]{0,2,1:T(8,128)(2,1)}), bf16[256,32,64]{0,2,1:T(8,128)(2,1)S(1)}, u32[]{:S(2)}, u32[]{:S(2)}) async-start(bf16[256,32,64]{0,2,1:T(8,128)(2,1)} %bitcast.40), calls=%async_computation.1 | async-start | bytes 2097152 | tf_op jit(solution)/shard_map/all_to_all | solution.py:37
  82.7 0.1 copy.24
  82.8 0.1 mul.49
  83.0 0.1 copy.27
  83.1 0.1 mul.56
  83.2 16.6 %all-to-all-done = bf16[256,32,64]{0,2,1:T(8,128)(2,1)S(1)} async-done(((bf16[256,32,64]{0,2,1:T(8,128)(2,1)}), bf16[256,32,64]{0,2,1:T(8,128)(2,1)S(1)}, u32[]{:S(2)}, u32[]{:S(2)}) %all-to-all-start) | async-done | bytes 1048608 | tf_op jit(solution)/shard_map/all_to_all | solution.py:37
  100.0 5.1 %fusion.11 = (f32[64,512]{1,0:T(8,128)S(1)}, f32[64,512]{1,0:T(8,128)S(1)}, f32[64,512]{1,0:T(8,128)S(1)}, f32[64,512]{1,0:T(8,128)S(1)}) fusion(f32[64,512]{1,0:T(8,128)S(1)} %bitcast.41, bf16[64,512]{1,0:T(8,128)(2,1)S(1)} %copy-done.1, f32[64,512]{1,0:T(8,128)S(1)} %bitcast.42, bf16[64,512]{1,0:T(8,128)(2,1)S(1)} %copy-done.2, ...), kind=kOutput, calls=%fused_computation.30 | convolution fusion | flops 537296896 | bytes 10354688 | tf_op jit(solution)/shard_map/dot_general | solution.py:41
  105.1 0.6 copy-done
  105.7 2.6 %convolution_convert_fusion = bf16[64,8192]{1,0:T(8,128)(2,1)S(1)} fusion(bf16[8192,512]{1,0:T(8,128)(2,1)S(1)} %copy-done, f32[64,512]{1,0:T(8,128)S(1)} %get-tuple-element.21, f32[64,512]{1,0:T(8,128)S(1)} %get-tuple-element.19), kind=kOutput, calls=%fused_computation.3 | convolution fusion | flops 537559040 | bytes 9699328 | tf_op jit(solution)/shard_map/dot_general | solution.py:58
  108.4 0.1 copy.39
  108.5 21.0 %all_to_all.38 = bf16[32,256,64]{1,2,0:T(8,128)(2,1)} all-to-all(bf16[32,256,64]{1,2,0:T(8,128)(2,1)S(1)} %bitcast.38), channel_id=1, replica_groups=mesh['replica'=4,'fsdp'=32] {'fsdp'}, dimensions={0} | all-to-all | bytes 2097152 | tf_op jit(solution)/shard_map/all_to_all | solution.py:61
  129.5 1.4 scatter_custom_fusion
  131.0 0.1 abs.13
  131.1 0.1 reduce_max.18
  131.2 0.6 copy.30
  131.9 0.1 div.42
  132.0 0.1 abs.15
  132.1 0.1 reduce_max.19
  132.3 0.6 copy.31
  132.9 0.1 div.45
  133.1 0.7 divide_convert_fusion
  133.8 39.9 %all-gather.5.cloned.1.call-done = bf16[256,8192]{0,1:T(8,128)(2,1)} async-done(((bf16[256,2048]{0,1:T(8,128)(2,1)}), bf16[256,8192]{0,1:T(8,128)(2,1)}) %all-gather.5.cloned.1.call-update) | async-done | bytes 4194320 | tf_op jit(solution)/shard_map/all_gather | solution.py:62
  173.7 5.0 %gather_fusion.1 = bf16[256,256,32]{1,2,0:T(8,128)(2,1)} fusion(bf16[256,256,32]{0,2,1:T(8,128)(2,1)} %bitcast.32, s32[1024]{0:T(1024)S(1)} %pad_clamp_fusion), kind=kCustom, calls=%fused_computation.1.clone | custom fusion | bytes 8389632 | tf_op jit(solution)/shard_map/jit(_take)/gather | solution.py:66
  178.7 4.0 %broadcast_select_fusion = bf16[256,256,32]{1,2,0:T(8,128)(2,1)} fusion(bf16[256,256,32]{1,2,0:T(8,128)(2,1)} %gather_fusion.1, pred[256]{0:T(512)(128)(4,1)S(1)} %compare_and_fusion), kind=kLoop, calls=%fused_computation.4 | loop fusion | flops 2097152 | bytes 8388864 | tf_op jit(solution)/shard_map/jit(_take)/select_n | solution.py:66
  182.7 6.3 %copy.29 = bf16[256,8192]{1,0:T(8,128)(2,1)} copy(bf16[256,8192]{0,1:T(8,128)(2,1)} %bitcast.34) | data formatting | bytes 8388608
  (27 shorter events, 0.3 us)
Async XLA Ops:
  8.0 67.0 %reduce-scatter.2.cloned.1.call-start = ((), (), s32[]{:S(2)}) async-start(), calls=%async_computation.3 | async-start | bytes 5242880 | tf_op jit(solution)/shard_map/reduce_scatter | solution.py:34
  24.8 57.9 %copy-start.3 = (f32[64,2]{0,1:T(2,128)S(1)}, f32[64,2]{0,1:T(2,128)}, u32[]{:S(2)}) copy-start(f32[64,2]{0,1:T(2,128)} %param.13) | copy-start | bytes 1540
  24.8 58.2 %copy-start.4 = (f32[64,2]{0,1:T(2,128)S(1)}, f32[64,2]{0,1:T(2,128)}, u32[]{:S(2)}) copy-start(f32[64,2]{0,1:T(2,128)} %param.15) | copy-start | bytes 1540
  24.8 75.2 %copy-start.1 = (bf16[64,512]{1,0:T(8,128)(2,1)S(1)}, bf16[64,512]{1,0:T(8,128)(2,1)}, u32[]{:S(2)}) copy-start(bf16[64,512]{1,0:T(8,128)(2,1)} %param.12) | copy-start | bytes 196612
  24.8 75.2 %copy-start.2 = (bf16[64,512]{1,0:T(8,128)(2,1)S(1)}, bf16[64,512]{1,0:T(8,128)(2,1)}, u32[]{:S(2)}) copy-start(bf16[64,512]{1,0:T(8,128)(2,1)} %param.14) | copy-start | bytes 196612
  24.8 75.1 %all-gather.3.cloned.1.call-start = ((), (), s32[]{:S(2)}) async-start(), calls=%async_computation.4 | async-start | bytes 8650752 | tf_op jit(solution)/shard_map/all_gather | solution.py:40
  75.0 24.8 %all-to-all-start = ((bf16[256,32,64]{0,2,1:T(8,128)(2,1)}), bf16[256,32,64]{0,2,1:T(8,128)(2,1)S(1)}, u32[]{:S(2)}, u32[]{:S(2)}) async-start(bf16[256,32,64]{0,2,1:T(8,128)(2,1)} %bitcast.40), calls=%async_computation.1 | async-start | bytes 2097152 | tf_op jit(solution)/shard_map/all_to_all | solution.py:37
  82.7 91.0 %all-gather.5.cloned.1.call-start = ((), (), s32[]{:S(2)}) async-start(), calls=%async_computation.5 | async-start | bytes 5242880 | tf_op jit(solution)/shard_map/all_gather | solution.py:62
  100.0 5.8 %copy-start = (bf16[8192,512]{1,0:T(8,128)(2,1)S(1)}, bf16[8192,512]{1,0:T(8,128)(2,1)}, u32[]{:S(2)}) copy-start(bf16[8192,512]{1,0:T(8,128)(2,1)} %all-gather.3.cloned.1.call-done) | copy-start | bytes 25165828
Sparse Core Ops, SparseCore 0:
  25.0 50.0 reduce-scatter.1
  129.6 43.9 all-gather.4
Sparse Core Ops, SparseCore 1:
  27.8 56.6 all-gather.2
where the time goes:
time: 197 us; the launch traced here: 196 us
  waiting for transfers between devices  107 us (54%)
  local copies, waits for them, and re-layouts  27.1 us (14%)
  blocking collectives  21 us (11%)
  between operations  15.7 us (8%)
  other arithmetic  10.4 us (5%)
  starting transfers between devices  7.77 us (4%)
  matrix products  7.74 us (4%)
    reduce_scatter x1, waiting for transfers between devices, local(): lax.psum_scatter(reordered, 'replica', scatter_dimension=1, tiled=True)  49.6 us
    all_gather x1, waiting for transfers between devices, local(): ordered = lax.all_gather(returned, 'replica', axis=1, tiled=True)  39.9 us
    all_to_all x1, blocking collectives, local(): lax.all_to_all(owner_block, 'fsdp', split_axis=0, concat_axis=1, tiled=True)  21 us
    all_to_all x1, waiting for transfers between devices, local(): lax.all_to_all(summed.astype(jnp.bfloat16), 'fsdp', split_axis=1, concat_...  16.6 us
    unnamed x20, local copies, waits for them, and re-layouts  14.8 us
    all_to_all x1, starting transfers between devices, local(): lax.all_to_all(summed.astype(jnp.bfloat16), 'fsdp', split_axis=1, concat_...  7.65 us
    dot_general x1, matrix products, local(): lax.dot_general(columns, proj_whole.astype(jnp.float32), (((0,), (0,)), (...  5.12 us
    gather x1, local copies, waits for them, and re-layouts, local(): jnp.take(ordered.reshape(row_count, panel_count, PW), inverse, axis=1)  5.02 us
  transfers between devices with their start and end apart: 4, of which 3 were waited for; matrix products, arithmetic and copies ran while one was open for 2% of the time, Pallas kernels for 0%

commit v1 on v0

v1 whole, which is shorter than its diff:
```python
import functools

import jax
import jax.numpy as jnp
from jax import lax
from jax.experimental import pallas as pl
from jax.experimental.pallas import tpu as pltpu
from jax.sharding import PartitionSpec as P

PW = 32
QB = 256
STEP = 2
RING = 4
LANES = 128

beta_one = 0.9
beta_two = 0.999
adam_eps = 1e-08
scale_eps = 1e-06

MESH = pl.DeviceIdType.MESH

CHIPS = RING**3
OWNED = 64
RANK = 512
PARTS = (
    (("x", "y", "z"), 96, 0),
    (("y", "z", "x"), 96, 96 * CHIPS),
    (("z", "x", "y"), 64, 192 * CHIPS),
)
HALF_ROWS = 256 * CHIPS


def block_row(part, chip):
    order, size, base = PARTS[part]
    a, b, c = (chip[name] for name in order)
    return base + ((a * RING + b) * RING + c) * size


def shifted(chip, axis, step):
    moved = dict(chip)
    moved[axis] = lax.rem(chip[axis] + step, RING)
    return moved


def device_of(chip, core):
    return (chip["x"], (chip["z"] * RING + chip["y"]) * 2 + core)


def rows(start, size):
    return pl.ds(pl.multiple_of(start, 32), size)


def owner_tiles(part):
    if part == 2:
        return [(slice(0, 64), slice(256, 384))]
    lanes = slice(part * 128, part * 128 + 128)
    return [(slice(0, 64), lanes), (slice(32 * part, 32 * part + 32), slice(384, 512))]


def put_block(ref, start, part, value, row_base=0):
    at = 0
    for row, lane in owner_tiles(part):
        size = row.stop - row.start
        ref[rows(start + at, size), :] = value[row_base + row.start : row_base + row.stop, lane].astype(ref.dtype)
        at += size


def kernel(
    plan_ref, table_ref, grad_hbm, proj_ref, fc_ref, fs_ref, sc_ref, ss_ref,
    update_hbm, ofc_ref, ofs_ref, osc_ref, oss_ref,
    grad_ref, turned, other_out, other_in, own_rows, proj_other,
    sums1, recv1, sums2, recv2, sums3, recv3, lowrank, whole, natural, update_ref,
    grad_sem, pair_send, pair_recv, rs_send, rs_recv, ag_send, ag_recv, fwd_send, fwd_recv, out_sem,
):
    replica = lax.axis_index("replica")
    inner = lax.axis_index("fsdp")
    chip = {"x": replica, "z": inner // 8, "y": lax.rem(inner // 2, RING)}
    core = lax.rem(inner, 2)
    other = 1 - core
    sibling = device_of(chip, other)
    cols = grad_hbm.shape[2] // RING

    loads = []
    for j in range(RING):
        loads.append(
            pltpu.make_async_copy(
                grad_hbm.at[0, :, pl.ds(j * cols, cols)], grad_ref.at[:, pl.ds(j * cols, cols)], grad_sem.at[j]
            )
        )
        loads[-1].start()

    barrier = pltpu.get_barrier_semaphore()
    pl.semaphore_signal(barrier, inc=1, device_id=sibling, device_id_type=MESH)
    for axis in ("x", "y", "z"):
        for step in range(1, RING):
            pl.semaphore_signal(
                barrier, inc=1, device_id=device_of(shifted(chip, axis, step), core), device_id_type=MESH
            )

    for j in range(RING):
        loads[j].wait()

        @pl.loop(0, cols // 256)
        def _(t, j=j):
            at = pl.multiple_of(j * cols + t * 256, 256)
            block = grad_ref[:, pl.ds(at, 256)].T
            turned[pl.ds(at // PW, 256 // PW)] = block.reshape(256 // PW, PW, block.shape[1])

    pl.semaphore_wait(barrier, 3 * (RING - 1) + 1)

    def remote(src, dst, send, recv, target):
        return pltpu.make_async_remote_copy(
            src_ref=src, dst_ref=dst, send_sem=send, recv_sem=recv, device_id=target, device_id_type=MESH
        )

    proj_copy = remote(proj_ref, proj_other, pair_send.at[RING], pair_recv.at[RING], sibling)
    proj_copy.start()

    def pick(target, which, first):
        @pl.loop(0, 32)
        def _(t):
            panel = first * 32 + t
            position = (panel // 2) * 4 + which * 2 + lax.rem(panel, 2)
            target[rows(panel * PW, PW), :] = turned[plan_ref[position]]

    pair = []
    span = CHIPS // RING * OWNED
    for j in range(RING):
        pick(other_out, other, j)
        part_rows = pl.ds(j * span, span)
        pair.append(
            remote(other_out.at[part_rows, :], other_in.at[part_rows, :], pair_send.at[j], pair_recv.at[j], sibling)
        )
        pair[-1].start()
    for j in range(RING):
        pick(own_rows, core, j)

    proj_copy.wait_recv()
    for j in range(RING):
        pair[j].wait_recv()

        @pl.loop(0, RING)
        def _(z, j=j):
            at = rows((j * RING + z) * RING * OWNED, RING * OWNED)
            product = jnp.dot(own_rows[at, :], proj_ref[...], preferred_element_type=jnp.float32)
            product += jnp.dot(other_in[at, :], proj_other[...], preferred_element_type=jnp.float32)
            for y in range(RING):
                for part in range(3):
                    put_block(sums1, block_row(part, {"x": j, "z": z, "y": y}), part, product, y * OWNED)

    def stage_copies(stage, source, landing, send, recv):
        copies = {}
        for part, (order, size, base) in enumerate(PARTS):
            unit = size * RING ** (2 - stage)
            origin = base // RING**stage
            landing_origin = 3 * base // RING ** (stage + 1)
            for step in range(1, RING):
                to = shifted(chip, order[stage], step)
                sem = stage * 9 + part * 3 + step - 1
                copies[part, step] = remote(
                    source.at[rows(origin + to[order[stage]] * unit, unit), :],
                    landing.at[pl.ds(landing_origin + (step - 1) * unit, unit), :],
                    send.at[sem],
                    recv.at[sem],
                    device_of(to, core),
                )
        return copies

    stages = [
        stage_copies(0, sums1, recv1, rs_send, rs_recv),
        stage_copies(1, sums2, recv2, rs_send, rs_recv),
        stage_copies(2, sums3, recv3, rs_send, rs_recv),
    ]
    sources = (sums1, sums2, sums3)
    landings = (recv1, recv2, recv3)

    for step in (2, 1, 3):
        for part in range(3):
            stages[0][part, step].start()

    for stage in (0, 1):
        for part, (order, size, base) in enumerate(PARTS):
            for step in range(1, RING):
                stages[stage][part, step].wait_recv()
            unit = size * RING ** (2 - stage)
            inner_unit = unit // RING
            own = base // RING**stage + chip[order[stage]] * unit
            landed = 3 * base // RING ** (stage + 1)
            target = base // RING ** (stage + 1)
            for step in (2, 1, 3, 0):
                slot = lax.rem(chip[order[stage + 1]] + step, RING)
                tile = min(inner_unit, 128 if size == 64 else 96)

                @pl.loop(0, inner_unit // tile)
                def _(t, own=own, landed=landed, target=target, slot=slot, unit=unit, inner_unit=inner_unit,
                      tile=tile, stage=stage):
                    at = slot * inner_unit + t * tile
                    total = sources[stage][rows(own + at, tile), :].astype(jnp.float32)
                    for i in range(3):
                        total += landings[stage][rows(landed + i * unit + at, tile), :].astype(jnp.float32)
                    sources[stage + 1][rows(target + at, tile), :] = total.astype(jnp.bfloat16)

                if step:
                    stages[stage + 1][part, step].start()

    for part, (order, size, base) in enumerate(PARTS):
        for step in range(1, RING):
            stages[2][part, step].wait_recv()
        total = sums3[rows(base // 16 + chip[order[2]] * size, size), :].astype(jnp.float32)
        for i in range(3):
            total += recv3[pl.ds(3 * base // 64 + i * size, size), :].astype(jnp.float32)
        at = 0
        for row, lane in owner_tiles(part):
            count = row.stop - row.start
            lowrank[row, lane] = total[at : at + count, :]
            at += count

    directions = []
    for b in range(RANK // QB):
        lane = slice(b * QB, (b + 1) * QB)
        low = lowrank[:, lane]
        first = fc_ref[:, lane].astype(jnp.float32) * fs_ref[:, b : b + 1]
        second = sc_ref[:, lane].astype(jnp.float32) * ss_ref[:, b : b + 1]
        first_new = beta_one * first + (1.0 - beta_one) * low
        second_new = beta_two * second + (1.0 - beta_two) * low * low
        corr_one = 1.0 - beta_one**STEP
        corr_two = 1.0 - beta_two**STEP
        directions.append(
            (first_new / corr_one / (jnp.sqrt(second_new / corr_two) + adam_eps)).astype(jnp.bfloat16)
        )
        for value, codes, scales in ((first_new, ofc_ref, ofs_ref), (second_new, osc_ref, oss_ref)):
            peak = jnp.max(jnp.abs(value), axis=1, keepdims=True) + scale_eps
            codes[:, lane] = (value / peak).astype(jnp.bfloat16)
            scales[:, b : b + 1] = peak
    direction = jnp.concatenate(directions, axis=1)

    mine = core * HALF_ROWS

    def in_whole(start, size):
        return pl.ds(start // PW, size // PW)

    for part in range(3):
        at = mine + block_row(part, chip)
        for row, lane in owner_tiles(part):
            size = row.stop - row.start
            whole[in_whole(at, size)] = direction[row, lane].reshape(size // PW, PW, LANES)
            at += size

    gathers, forwards = {}, []

    def forward(part, index, start, size):
        where = whole.at[in_whole(start, size)]
        forwards.append(
            remote(where, where, fwd_send.at[part * 7 + index], fwd_recv.at[part * 7 + index], sibling)
        )
        forwards[-1].start()

    def stage_start(part, stage):
        order, size, base = PARTS[part]
        unit = size * RING ** (2 - stage)
        at = dict(chip)
        for name in order[stage + 1 :]:
            at[name] = 0
        where = whole.at[in_whole(mine + block_row(part, at), unit)]
        for step in (2, 1, 3):
            sem = stage * 9 + part * 3 + step - 1
            gathers[part, stage, step] = remote(
                where, where, ag_send.at[sem], ag_recv.at[sem], device_of(shifted(chip, order[stage], step), core)
            )
            gathers[part, stage, step].start()

    def stage_landed(part, stage, step):
        order, size, base = PARTS[part]
        unit = size * RING ** (2 - stage)
        at = shifted(chip, order[stage], RING - step)
        for name in order[stage + 1 :]:
            at[name] = 0
        start = mine + block_row(part, at)
        where = whole.at[in_whole(start, unit)]
        sem = stage * 9 + part * 3 + step - 1
        remote(where, where, ag_send.at[sem], ag_recv.at[sem], sibling).wait_recv()
        return start, unit

    for part in range(3):
        stage_start(part, 2)
    for part in range(3):
        order, size, base = PARTS[part]
        for step in range(1, RING):
            stage_landed(part, 2, step)
        stage_start(part, 1)
        at = dict(chip)
        at[order[2]] = 0
        forward(part, 0, mine + block_row(part, at), size * RING)
    for part in range(3):
        landed = [stage_landed(part, 1, step) for step in range(1, RING)]
        stage_start(part, 0)
        for i, (start, unit) in enumerate(landed):
            forward(part, 1 + i, start, unit)
    for step in (1, 3, 2):
        for part in range(3):
            start, unit = stage_landed(part, 0, step)
            forward(part, 3 + step, start, unit)
    theirs = other * HALF_ROWS
    for part, (order, size, base) in enumerate(PARTS):
        at = dict(chip)
        at[order[2]] = 0
        waits = [(0, at, size * RING)]
        for step in range(1, RING):
            at = shifted(chip, order[1], RING - step)
            at[order[2]] = 0
            waits.append((step, at, size * RING))
            at = shifted(chip, order[0], RING - step)
            at[order[1]] = 0
            at[order[2]] = 0
            waits.append((3 + step, at, size * RING * RING))
        for index, at, unit in waits:
            where = whole.at[in_whole(theirs + block_row(part, at), unit)]
            sem = part * 7 + index
            remote(where, where, fwd_send.at[sem], fwd_recv.at[sem], sibling).wait_recv()

    tile = 512
    steps = update_ref.shape[1] // tile

    @pl.loop(0, steps)
    def _(t):
        for p in range(tile // PW):
            for lane in range(4):
                source = table_ref[lane * 256 + t * (tile // PW) + p]
                natural[p * PW : (p + 1) * PW, lane * LANES : (lane + 1) * LANES] = whole[source]
        product = lax.dot_general(
            proj_ref[...], natural[...], (((1,), (1,)), ((), ())), preferred_element_type=jnp.float32
        )
        update_ref[:, pl.ds(pl.multiple_of(t * tile, tile), tile)] = product.astype(jnp.bfloat16)

    store = pltpu.make_async_copy(update_ref, update_hbm, out_sem)
    store.start()

    proj_copy.wait_send()
    for copy in pair:
        copy.wait_send()
    for stage in stages:
        for copy in stage.values():
            copy.wait_send()
    for copy in gathers.values():
        copy.wait_send()
    for copy in forwards:
        copy.wait_send()
    store.wait()


def local(gradients, projection, plan, first_codes, first_scales, second_codes, second_scales):
    panel_count = plan.shape[0]
    position = jnp.arange(panel_count, dtype=jnp.int32)
    owner = position // 2
    half = position % 2
    chip = {"x": owner // 32, "z": owner // 8 % RING, "y": owner // 2 % RING}
    base = (owner % 2) * HALF_ROWS
    starts = [base + block_row(part, chip) for part in range(3)]
    table = jnp.stack(
        [start + half * PW for start in starts] + [jnp.where(half == 0, starts[0], starts[1]) + 64]
    )
    found = plan[None, :] == position[:, None]
    table = jnp.sum(jnp.where(found[None], table[:, None, :] // PW, 0), axis=2).reshape(-1)

    bf16, f32 = jnp.bfloat16, jnp.float32
    vmem = pl.BlockSpec(memory_space=pltpu.VMEM)
    smem = pl.BlockSpec(memory_space=pltpu.SMEM)
    hbm = pl.BlockSpec(memory_space=pl.ANY)
    sem = pltpu.SemaphoreType.DMA
    rows_count, col_count = gradients.shape[1:]
    half_cols = col_count // 2
    return pl.pallas_call(
        kernel,
        out_shape=(
            jax.ShapeDtypeStruct((rows_count, col_count), bf16),
            jax.ShapeDtypeStruct(first_codes.shape, bf16),
            jax.ShapeDtypeStruct(first_scales.shape, f32),
            jax.ShapeDtypeStruct(second_codes.shape, bf16),
            jax.ShapeDtypeStruct(second_scales.shape, f32),
        ),
        in_specs=[smem, smem, hbm, vmem, vmem, vmem, vmem, vmem],
        out_specs=(hbm, vmem, vmem, vmem, vmem),
        scratch_shapes=[
            pltpu.VMEM((rows_count, col_count), bf16),
            pltpu.VMEM((col_count // PW, PW, rows_count), bf16),
            pltpu.VMEM((half_cols, rows_count), bf16),
            pltpu.VMEM((half_cols, rows_count), bf16),
            pltpu.VMEM((half_cols, rows_count), bf16),
            pltpu.VMEM(projection.shape, bf16),
            pltpu.VMEM((HALF_ROWS, LANES), bf16),
            pltpu.VMEM((HALF_ROWS * 3 // 4, LANES), bf16),
            pltpu.VMEM((HALF_ROWS // 4, LANES), bf16),
            pltpu.VMEM((HALF_ROWS * 3 // 16, LANES), bf16),
            pltpu.VMEM((HALF_ROWS // 16, LANES), bf16),
            pltpu.VMEM((HALF_ROWS * 3 // 64, LANES), bf16),
            pltpu.VMEM(first_codes.shape, f32),
            pltpu.VMEM((2 * HALF_ROWS // PW, PW, LANES), bf16),
            pltpu.VMEM((512, RANK), bf16),
            pltpu.VMEM((rows_count, col_count), bf16),
            sem((4,)), sem((5,)), sem((5,)), sem((27,)), sem((27,)), sem((27,)), sem((27,)), sem((21,)), sem((21,)),
            sem,
        ],
        compiler_params=pltpu.CompilerParams(
            collective_id=0, has_side_effects=True, vmem_limit_bytes=60 * 1024 * 1024
        ),
    )(plan, table, gradients, projection, first_codes, first_scales, second_codes, second_scales)


def solution(mesh):
    in_specs = (
        P("replica", "fsdp", None),
        P("fsdp", None),
        P(),
        P(("replica", "fsdp"), None),
        P(("replica", "fsdp"), None),
        P(("replica", "fsdp"), None),
        P(("replica", "fsdp"), None),
    )
    out_specs = (
        P("fsdp", None),
        P(("replica", "fsdp"), None),
        P(("replica", "fsdp"), None),
        P(("replica", "fsdp"), None),
        P(("replica", "fsdp"), None),
    )
    return jax.shard_map(local, mesh=mesh, in_specs=in_specs, out_specs=out_specs, check_vma=False)
```

time: 197 us -> 105 us (0.53)
  waiting for transfers between devices: 107 us -> 0 us
  Pallas kernels: 0 us -> 90.4 us
  blocking collectives: 21 us -> 0 us
  between operations: 15.7 us -> 0.67 us
  local copies, waits for them, and re-layouts: 27.1 us -> 12.1 us
  other arithmetic: 10.4 us -> 1.02 us
  starting transfers between devices: 7.77 us -> 0 us
  matrix products: 7.74 us -> 0 us
    pallas_call x0 -> x1, Pallas kernels: none -> 90.4 us  [local(): pl.pallas_call(kernel, out_shape=(jax.ShapeDtypeStruct((rows_count, col_c...]
    reduce_scatter x1 -> x0, waiting for transfers between devices: 49.6 us -> none  [local(): lax.psum_scatter(reordered, 'replica', scatter_dimension=1, tiled=True)]
    all_gather x2 -> x0, waiting for transfers between devices: 39.9 us -> none  [the longest x1 39.9 us: local(): ordered = lax.all_gather(returned, 'replica', axis=1, tiled=True)]
    all_to_all x1 -> x0, blocking collectives: 21 us -> none  [local(): lax.all_to_all(owner_block, 'fsdp', split_axis=0, concat_axis=1, tiled=True)]
    all_to_all x1 -> x0, waiting for transfers between devices: 16.6 us -> none  [local(): lax.all_to_all(summed.astype(jnp.bfloat16), 'fsdp', split_axis=1, concat_...]
    gather x2 -> x0, local copies, waits for them, and re-layouts: 9.97 us -> none  [the longest x1 5.02 us: local(): jnp.take(ordered.reshape(row_count, panel_count, PW), inverse, axis=1)]
    select_n x4 -> x1, other arithmetic: 8.73 us -> 0.02 us  [local(): table[:, None, :] // PW]
    dot_general x2 -> x0, matrix products: 7.74 us -> none  [the longest x1 5.12 us: local(): lax.dot_general(columns, proj_whole.astype(jnp.float32), (((0,), (0,)), (...]
  transfers between devices with their start and end apart: 4 -> 0, of which waited for: 3 -> 0; matrix products, arithmetic and copies ran while one was open for 2% -> 0% of each run, Pallas kernels for 0% -> 0%
where the time goes in v1:
time: 105 us; the launch traced here: 104 us
  Pallas kernels  90.4 us (86%)
  local copies, waits for them, and re-layouts  12.1 us (12%)
    pallas_call x1, Pallas kernels, local(): pl.pallas_call(kernel, out_shape=(jax.ShapeDtypeStruct((rows_count, col_c...  90.4 us
    unnamed x10, local copies, waits for them, and re-layouts  9.31 us
    pallas_call x2, local copies, waits for them, and re-layouts, local(): pl.pallas_call(kernel, out_shape=(jax.ShapeDtypeStruct((rows_count, col_c...  2.79 us

profile of v1, /device:TPU:1, one launch (start us, length us, event | category | flops | bytes accessed | tf_op | source)
XLA Modules:
  0.0 104.2 jit_solution(14902843661388602506)
XLA Ops:
  0.7 1.4 %copy.16.fs_ref = f32[64,2]{1,0:T(8,128)} copy(f32[64,2]{0,1:T(2,128)} %param.11) | data formatting | bytes 1024 | tf_op args[4]
  2.1 1.4 %copy.17.ss_ref = f32[64,2]{1,0:T(8,128)} copy(f32[64,2]{0,1:T(2,128)} %param.13) | data formatting | bytes 1024 | tf_op args[6]
  3.5 0.7 iota_compare_fusion
  4.2 0.2 select_reduce_fusion
  4.4 0.6 copy.20
  5.0 90.4 %shard_map.110 = (bf16[256,8192]{1,0:T(8,128)(2,1)}, bf16[64,512]{1,0:T(8,128)(2,1)}, f32[64,2]{1,0:T(8,128)}, bf16[64,512]{1,0:T(8,128)(2,1)}, f32[64,2]{1,0:T(8,128)}) custom-call(s32[256]{0:T(256)} %plan_ref.1, s32[1024]{0:T(1024)} %bitcast.3, bf16[1,256,8192]{2,1,0:T(8,128)(2,1)} %grad_hbm.1, bf16[256,512]{1,0:T(8,128)(2,1)} %proj_ref.1, ...), custom_call_target="tpu_custom_call" | custom-call | tf_op jit(solution)/shard_map/pallas_call | solution.py:373
  95.5 1.4 %copy.18 = f32[64,2]{0,1:T(2,128)} copy(f32[64,2]{1,0:T(8,128)} %get-tuple-element.12) | data formatting | bytes 1024 | tf_op jit(solution)/shard_map/pallas_call | solution.py:373
  96.9 1.4 %copy.19 = f32[64,2]{0,1:T(2,128)} copy(f32[64,2]{1,0:T(8,128)} %get-tuple-element.14) | data formatting | bytes 1024 | tf_op jit(solution)/shard_map/pallas_call | solution.py:373
  98.3 0.0 copy-start.1
  98.3 0.0 copy-start
  98.3 4.7 %copy.24 = bf16[256,8192]{1,0:T(8,128)(2,1)} copy(bf16[256,8192]{1,0:T(8,128)(2,1)} %get-tuple-element.24) | data formatting | bytes 8388608
  103.0 0.0 copy-done.1
  103.0 0.6 copy.25
  103.6 0.0 copy-done
  103.6 0.6 copy.26
  (3 shorter events, 0.1 us)
Async XLA Ops:
  98.3 4.7 %copy-start.1 = (bf16[64,512]{1,0:T(8,128)(2,1)S(1)}, bf16[64,512]{1,0:T(8,128)(2,1)}, u32[]{:S(2)}) copy-start(bf16[64,512]{1,0:T(8,128)(2,1)} %get-tuple-element.25) | copy-start | bytes 196612
  98.3 5.3 %copy-start = (bf16[64,512]{1,0:T(8,128)(2,1)S(1)}, bf16[64,512]{1,0:T(8,128)(2,1)}, u32[]{:S(2)}) copy-start(bf16[64,512]{1,0:T(8,128)(2,1)} %get-tuple-element.27) | copy-start | bytes 196612

commit v2 on v1

v2 whole, which is shorter than its diff:
```python
import functools

import jax
import jax.numpy as jnp
from jax import lax
from jax.experimental import pallas as pl
from jax.experimental.pallas import tpu as pltpu
from jax.sharding import PartitionSpec as P

PW = 32
QB = 256
STEP = 2
RING = 4
LANES = 128

beta_one = 0.9
beta_two = 0.999
adam_eps = 1e-08
scale_eps = 1e-06

MESH = pl.DeviceIdType.MESH

CHIPS = RING**3
OWNED = 64
RANK = 512
PARTS = (
    (("x", "y", "z"), 96, 0),
    (("y", "z", "x"), 96, 96 * CHIPS),
    (("z", "x", "y"), 64, 192 * CHIPS),
)
HALF_ROWS = 256 * CHIPS
RS_SETS = ((1, 0), (2, 3))
AG_SETS = ((0, 1), (3, 2))


def block_row(part, chip):
    order, size, base = PARTS[part]
    a, b, c = (chip[name] for name in order)
    return base + ((a * RING + b) * RING + c) * size


def shifted(chip, axis, step):
    moved = dict(chip)
    moved[axis] = lax.rem(chip[axis] + step, RING)
    return moved


def device_of(chip, core):
    return (chip["x"], (chip["z"] * RING + chip["y"]) * 2 + core)


def rows(start, size):
    return pl.ds(pl.multiple_of(start, 32), size)


def owner_tiles(part):
    if part == 2:
        return [(slice(0, 64), slice(256, 384))]
    lanes = slice(part * 128, part * 128 + 128)
    return [(slice(0, 64), lanes), (slice(32 * part, 32 * part + 32), slice(384, 512))]


def put_block(ref, start, part, value, row_base=0):
    at = 0
    for row, lane in owner_tiles(part):
        size = row.stop - row.start
        ref[rows(start + at, size), :] = value[row_base + row.start : row_base + row.stop, lane].astype(ref.dtype)
        at += size


def kernel(
    plan_ref, table_ref, grad_hbm, proj_ref, fc_ref, fs_ref, sc_ref, ss_ref,
    update_hbm, ofc_ref, ofs_ref, osc_ref, oss_ref,
    grad_ref, turned, other_out, other_in, own_rows, proj_other,
    sums1, transit, recv1, sums2, recv2, sums3, recv3, lowrank, whole, natural, update_ref,
    grad_sem, pair_send, pair_recv, first_send, first_recv, rs_send, rs_recv, near_send, near_recv, ag_send, ag_recv, fwd_send, fwd_recv, out_sem,
):
    replica = lax.axis_index("replica")
    inner = lax.axis_index("fsdp")
    chip = {"x": replica, "z": inner // 8, "y": lax.rem(inner // 2, RING)}
    core = lax.rem(inner, 2)
    other = 1 - core
    sibling = device_of(chip, other)
    cols = grad_hbm.shape[2] // RING

    loads = []
    for j in range(RING):
        loads.append(
            pltpu.make_async_copy(
                grad_hbm.at[0, :, pl.ds(j * cols, cols)], grad_ref.at[:, pl.ds(j * cols, cols)], grad_sem.at[j]
            )
        )
        loads[-1].start()

    barrier = pltpu.get_barrier_semaphore()
    pl.semaphore_signal(barrier, inc=1, device_id=sibling, device_id_type=MESH)
    for axis in ("x", "y", "z"):
        for step in range(1, RING):
            pl.semaphore_signal(
                barrier, inc=1, device_id=device_of(shifted(chip, axis, step), core), device_id_type=MESH
            )

    for j in range(RING):
        loads[j].wait()

        @pl.loop(0, cols // 256)
        def _(t, j=j):
            at = pl.multiple_of(j * cols + t * 256, 256)
            block = grad_ref[:, pl.ds(at, 256)].T
            turned[pl.ds(at // PW, 256 // PW)] = block.reshape(256 // PW, PW, block.shape[1])

    pl.semaphore_wait(barrier, 3 * (RING - 1) + 1)

    def remote(src, dst, send, recv, target):
        return pltpu.make_async_remote_copy(
            src_ref=src, dst_ref=dst, send_sem=send, recv_sem=recv, device_id=target, device_id_type=MESH
        )

    proj_copy = remote(proj_ref, proj_other, pair_send.at[RING], pair_recv.at[RING], sibling)
    proj_copy.start()

    def pick(target, which, first):
        @pl.loop(0, 32)
        def _(t):
            panel = first * 32 + t
            position = (panel // 2) * 4 + which * 2 + lax.rem(panel, 2)
            target[rows(panel * PW, PW), :] = turned[plan_ref[position]]

    pair = []
    span = CHIPS // RING * OWNED
    for j in range(RING):
        pick(other_out, other, j)
        part_rows = pl.ds(j * span, span)
        pair.append(
            remote(other_out.at[part_rows, :], other_in.at[part_rows, :], pair_send.at[j], pair_recv.at[j], sibling)
        )
        pair[-1].start()
    for j in range(RING):
        pick(own_rows, core, j)

    proj_copy.wait_recv()
    for j in range(RING):
        pair[j].wait_recv()

        @pl.loop(0, RING)
        def _(z, j=j):
            at = rows((j * RING + z) * RING * OWNED, RING * OWNED)
            product = jnp.dot(own_rows[at, :], proj_ref[...], preferred_element_type=jnp.float32)
            product += jnp.dot(other_in[at, :], proj_other[...], preferred_element_type=jnp.float32)
            for y in range(RING):
                for part in range(3):
                    put_block(sums1, block_row(part, {"x": j, "z": z, "y": y}), part, product, y * OWNED)

    def sub_row(part, a, b):
        order, size, base = PARTS[part]
        return block_row(part, {order[0]: a, order[1]: b, order[2]: 0})

    opening = {}
    for k in range(2):
        for part, (order, size, base) in enumerate(PARTS):
            a, b = chip[order[0]], chip[order[1]]
            sub = size * RING
            for way, flow in enumerate((1, RING - 1)):
                off = RS_SETS[way][k]
                b_to = lax.rem(b + off, RING)
                onward = device_of(shifted(chip, order[0], flow), core)
                backward = device_of(shifted(chip, order[0], RING - flow), core)
                sem = part * 4 + way * 2 + k
                slot = base // 4 + (way * 2 + k) * sub
                land = base // 2 + off * 2 * sub
                opening["far", part, way, k] = remote(
                    sums1.at[rows(sub_row(part, lax.rem(a + 2, RING), b_to), sub), :],
                    transit.at[pl.ds(slot, sub), :],
                    first_send.at[sem], first_recv.at[sem], onward,
                )
                opening["raw", part, way, k] = remote(
                    sums1.at[rows(sub_row(part, lax.rem(a + RING - flow, RING), b_to), sub), :],
                    recv1.at[pl.ds(land, sub), :],
                    first_send.at[12 + sem], first_recv.at[12 + sem], backward,
                )
                opening["both", part, way, k] = remote(
                    sums1.at[rows(sub_row(part, lax.rem(a + flow, RING), b_to), sub), :],
                    recv1.at[pl.ds(land + sub, sub), :],
                    first_send.at[24 + sem], first_recv.at[24 + sem], onward,
                )

    def first_start(kind, k):
        for part in range(3):
            for way in range(2):
                opening[kind, part, way, k].start()

    first_start("far", 0)
    first_start("far", 1)
    for k in range(2):
        first_start("raw", k)
        for part, (order, size, base) in enumerate(PARTS):
            for way, flow in enumerate((1, RING - 1)):
                opening["far", part, way, k].wait_recv()
                own = sub_row(
                    part,
                    lax.rem(chip[order[0]] + flow, RING),
                    lax.rem(chip[order[1]] + RS_SETS[way][k], RING),
                )
                slot = base // 4 + (way * 2 + k) * size * RING

                @pl.loop(0, RING)
                def _(t, own=own, slot=slot, size=size):
                    at = rows(own + t * size, size)
                    total = sums1[at, :].astype(jnp.float32)
                    total += transit[rows(slot + t * size, size), :].astype(jnp.float32)
                    sums1[at, :] = total.astype(jnp.bfloat16)

                opening["both", part, way, k].start()

    def stage_copies(stage, source, landing):
        copies = {}
        for part, (order, size, base) in enumerate(PARTS):
            unit = size * RING ** (2 - stage)
            origin = base // RING**stage
            landing_origin = 3 * base // RING ** (stage + 1)
            for step in range(1, RING):
                to = shifted(chip, order[stage], step)
                sem = (stage - 1) * 9 + part * 3 + step - 1
                copies[part, step] = remote(
                    source.at[rows(origin + to[order[stage]] * unit, unit), :],
                    landing.at[pl.ds(landing_origin + (step - 1) * unit, unit), :],
                    rs_send.at[sem],
                    rs_recv.at[sem],
                    device_of(to, core),
                )
        return copies

    middle, closing = stage_copies(1, sums2, recv2), stage_copies(2, sums3, recv3)

    for k in range(2):
        for part, (order, size, base) in enumerate(PARTS):
            a, b = chip[order[0]], chip[order[1]]
            sub = size * RING
            for way in range(2):
                off = RS_SETS[way][k]
                b_to = lax.rem(b + off, RING)
                own = sub_row(part, a, b_to)
                land = base // 2 + off * 2 * sub
                target = base // RING + b_to * sub
                opening["raw", part, way, k].wait_recv()
                opening["both", part, way, k].wait_recv()

                @pl.loop(0, RING)
                def _(t, own=own, land=land, target=target, sub=sub, size=size):
                    total = sums1[rows(own + t * size, size), :].astype(jnp.float32)
                    total += recv1[rows(land + t * size, size), :].astype(jnp.float32)
                    total += recv1[rows(land + sub + t * size, size), :].astype(jnp.float32)
                    sums2[rows(target + t * size, size), :] = total.astype(jnp.bfloat16)

                if off:
                    middle[part, off].start()

    for part, (order, size, base) in enumerate(PARTS):
        for step in range(1, RING):
            middle[part, step].wait_recv()
        unit = size * RING
        own = base // RING + chip[order[1]] * unit
        landed = 3 * base // RING**2
        target = base // RING**2
        for step in (2, 1, 3, 0):
            at = lax.rem(chip[order[2]] + step, RING) * size
            total = sums2[rows(own + at, size), :].astype(jnp.float32)
            for i in range(3):
                total += recv2[rows(landed + i * unit + at, size), :].astype(jnp.float32)
            sums3[rows(target + at, size), :] = total.astype(jnp.bfloat16)
            if step:
                closing[part, step].start()

    for part, (order, size, base) in enumerate(PARTS):
        for step in range(1, RING):
            closing[part, step].wait_recv()
        total = sums3[rows(base // 16 + chip[order[2]] * size, size), :].astype(jnp.float32)
        for i in range(3):
            total += recv3[pl.ds(3 * base // 64 + i * size, size), :].astype(jnp.float32)
        at = 0
        for row, lane in owner_tiles(part):
            count = row.stop - row.start
            lowrank[row, lane] = total[at : at + count, :]
            at += count

    first_scales, second_scales = fs_ref[...].T, ss_ref[...].T
    directions, peaks = [], []
    for b in range(RANK // QB):
        lane = slice(b * QB, (b + 1) * QB)
        low = lowrank[:, lane]
        first = fc_ref[:, lane].astype(jnp.float32) * first_scales[:, b : b + 1]
        second = sc_ref[:, lane].astype(jnp.float32) * second_scales[:, b : b + 1]
        first_new = beta_one * first + (1.0 - beta_one) * low
        second_new = beta_two * second + (1.0 - beta_two) * low * low
        corr_one = 1.0 - beta_one**STEP
        corr_two = 1.0 - beta_two**STEP
        directions.append(
            (first_new / corr_one / (jnp.sqrt(second_new / corr_two) + adam_eps)).astype(jnp.bfloat16)
        )
        for value, codes in ((first_new, ofc_ref), (second_new, osc_ref)):
            peak = jnp.max(jnp.abs(value), axis=1, keepdims=True) + scale_eps
            codes[:, lane] = (value / peak).astype(jnp.bfloat16)
            peaks.append(peak)
    direction = jnp.concatenate(directions, axis=1)
    ofs_ref[...] = jnp.concatenate(peaks[0::2], axis=1).T
    oss_ref[...] = jnp.concatenate(peaks[1::2], axis=1).T

    mine = core * HALF_ROWS

    def in_whole(start, size):
        return pl.ds(start // PW, size // PW)

    for part in range(3):
        at = mine + block_row(part, chip)
        for row, lane in owner_tiles(part):
            size = row.stop - row.start
            whole[in_whole(at, size)] = direction[row, lane].reshape(size // PW, PW, LANES)
            at += size

    started, forwards = [], []

    def copy_of(start, size, send, recv, target):
        where = whole.at[in_whole(start, size)]
        return remote(where, where, send, recv, target)

    def spread(start, size, send, recv, target):
        started.append(copy_of(mine + start, size, send, recv, target))
        started[-1].start()

    def forward(start, size):
        index = len(forwards)
        forwards.append((start, size))
        spread(start, size, fwd_send.at[index], fwd_recv.at[index], sibling)

    def landed(start, size, recv):
        copy_of(mine + start, size, first_send.at[0], recv, sibling).wait_recv()
        return start, size

    def sub_of(part, a_off, off):
        order, size, base = PARTS[part]
        start = sub_row(
            part, lax.rem(chip[order[0]] + a_off, RING), lax.rem(chip[order[1]] + off, RING)
        )
        return start, size * RING

    def near_start(part, off):
        order = PARTS[part][0]
        for way, flow in enumerate((1, RING - 1)):
            sem = 12 * way + part * 4 + off
            to = device_of(shifted(chip, order[0], flow), core)
            spread(*sub_of(part, 0, off), near_send.at[sem], near_recv.at[sem], to)

    def near_landed(part, off):
        order = PARTS[part][0]
        for way, flow in enumerate((1, RING - 1)):
            piece = landed(*sub_of(part, RING - flow, off), near_recv.at[12 * way + part * 4 + off])
            if off in AG_SETS[way]:
                sem = 24 + part * 4 + off
                to = device_of(shifted(chip, order[0], flow), core)
                spread(*piece, near_send.at[sem], near_recv.at[sem], to)
            forward(*piece)

    for part, (order, size, base) in enumerate(PARTS):
        for step in (2, 1, 3):
            sem = 9 + part * 3 + step - 1
            to = device_of(shifted(chip, order[2], step), core)
            spread(block_row(part, chip), size, ag_send.at[sem], ag_recv.at[sem], to)
    for part, (order, size, base) in enumerate(PARTS):
        for step in range(1, RING):
            landed(block_row(part, shifted(chip, order[2], RING - step)), size, ag_recv.at[9 + part * 3 + step - 1])
        piece = sub_of(part, 0, 0)
        for step in (2, 1, 3):
            sem = part * 3 + step - 1
            spread(*piece, ag_send.at[sem], ag_recv.at[sem], device_of(shifted(chip, order[1], step), core))
        near_start(part, 0)
        forward(*piece)

    def second_landed(part, step):
        off = RING - step
        piece = landed(*sub_of(part, 0, off), ag_recv.at[part * 3 + step - 1])
        near_start(part, off)
        forward(*piece)

    for step in (1, 3):
        for part in range(3):
            second_landed(part, step)
    for part in range(3):
        near_landed(part, 0)
    for part in range(3):
        second_landed(part, 2)
    for off in (3, 1, 2):
        for part in range(3):
            near_landed(part, off)
    for off in (0, 3, 1, 2):
        for part in range(3):
            forward(*landed(*sub_of(part, 2, off), near_recv.at[24 + part * 4 + off]))
    theirs = other * HALF_ROWS
    for index, (start, size) in enumerate(forwards):
        copy_of(theirs + start, size, first_send.at[0], fwd_recv.at[index], sibling).wait_recv()

    tile = 512
    steps = update_ref.shape[1] // tile

    @pl.loop(0, steps)
    def _(t):
        for p in range(tile // PW):
            packed = table_ref[t * (tile // PW) + p]
            half = lax.shift_right_logical(packed, 30)
            starts = [lax.shift_right_logical(packed, 10 * part) & 1023 for part in range(3)]
            sources = [start + half for start in starts] + [starts[0] + 2 + half * (starts[1] - starts[0])]
            for lane, source in enumerate(sources):
                natural[p * PW : (p + 1) * PW, lane * LANES : (lane + 1) * LANES] = whole[source]
        product = lax.dot_general(
            proj_ref[...], natural[...], (((1,), (1,)), ((), ())), preferred_element_type=jnp.float32
        )
        update_ref[:, pl.ds(pl.multiple_of(t * tile, tile), tile)] = product.astype(jnp.bfloat16)

    store = pltpu.make_async_copy(update_ref, update_hbm, out_sem)
    store.start()

    proj_copy.wait_send()
    for copy in pair:
        copy.wait_send()
    for stage in (opening, middle, closing):
        for copy in stage.values():
            copy.wait_send()
    for copy in started:
        copy.wait_send()
    store.wait()


def local(gradients, projection, plan, first_codes, first_scales, second_codes, second_scales):
    panel_count = plan.shape[0]
    position = jnp.arange(panel_count, dtype=jnp.int32)
    owner = position // 2
    half = position % 2
    chip = {"x": owner // 32, "z": owner // 8 % RING, "y": owner // 2 % RING}
    base = (owner % 2) * HALF_ROWS
    starts = [base + block_row(part, chip) for part in range(3)]
    starts = [start // PW for start in starts]
    packed = starts[0] + starts[1] * 1024 + starts[2] * 1024 * 1024 + half * 1024 * 1024 * 1024
    found = plan[None, :] == position[:, None]
    table = jnp.sum(jnp.where(found, packed[None, :], 0), axis=1)

    bf16, f32 = jnp.bfloat16, jnp.float32
    vmem = pl.BlockSpec(memory_space=pltpu.VMEM)
    smem = pl.BlockSpec(memory_space=pltpu.SMEM)
    hbm = pl.BlockSpec(memory_space=pl.ANY)
    sem = pltpu.SemaphoreType.DMA
    rows_count, col_count = gradients.shape[1:]
    half_cols = col_count // 2
    update, first_out, first_peak, second_out, second_peak = pl.pallas_call(
        kernel,
        out_shape=(
            jax.ShapeDtypeStruct((rows_count, col_count), bf16),
            jax.ShapeDtypeStruct(first_codes.shape, bf16),
            jax.ShapeDtypeStruct(first_scales.shape[::-1], f32),
            jax.ShapeDtypeStruct(second_codes.shape, bf16),
            jax.ShapeDtypeStruct(second_scales.shape[::-1], f32),
        ),
        in_specs=[smem, smem, hbm, vmem, vmem, vmem, vmem, vmem],
        out_specs=(hbm, vmem, vmem, vmem, vmem),
        scratch_shapes=[
            pltpu.VMEM((rows_count, col_count), bf16),
            pltpu.VMEM((col_count // PW, PW, rows_count), bf16),
            pltpu.VMEM((half_cols, rows_count), bf16),
            pltpu.VMEM((half_cols, rows_count), bf16),
            pltpu.VMEM((half_cols, rows_count), bf16),
            pltpu.VMEM(projection.shape, bf16),
            pltpu.VMEM((HALF_ROWS, LANES), bf16),
            pltpu.VMEM((HALF_ROWS // 4, LANES), bf16),
            pltpu.VMEM((HALF_ROWS // 2, LANES), bf16),
            pltpu.VMEM((HALF_ROWS // 4, LANES), bf16),
            pltpu.VMEM((HALF_ROWS * 3 // 16, LANES), bf16),
            pltpu.VMEM((HALF_ROWS // 16, LANES), bf16),
            pltpu.VMEM((HALF_ROWS * 3 // 64, LANES), bf16),
            pltpu.VMEM(first_codes.shape, f32),
            pltpu.VMEM((2 * HALF_ROWS // PW, PW, LANES), bf16),
            pltpu.VMEM((512, RANK), bf16),
            pltpu.VMEM((rows_count, col_count), bf16),
            sem((4,)), sem((5,)), sem((5,)), sem((36,)), sem((36,)), sem((18,)), sem((18,)), sem((36,)), sem((36,)),
            sem((18,)), sem((18,)), sem((48,)), sem((48,)), sem,
        ],
        compiler_params=pltpu.CompilerParams(
            collective_id=0, has_side_effects=True, vmem_limit_bytes=60 * 1024 * 1024
        ),
    )(plan, table, gradients, projection, first_codes, first_scales.T, second_codes, second_scales.T)
    return update, first_out, first_peak.T, second_out, second_peak.T


def solution(mesh):
    in_specs = (
        P("replica", "fsdp", None),
        P("fsdp", None),
        P(),
        P(("replica", "fsdp"), None),
        P(("replica", "fsdp"), None),
        P(("replica", "fsdp"), None),
        P(("replica", "fsdp"), None),
    )
    out_specs = (
        P("fsdp", None),
        P(("replica", "fsdp"), None),
        P(("replica", "fsdp"), None),
        P(("replica", "fsdp"), None),
        P(("replica", "fsdp"), None),
    )
    return jax.shard_map(local, mesh=mesh, in_specs=in_specs, out_specs=out_specs, check_vma=False)
```

time: 105 us -> 90 us (0.86)
  Pallas kernels: 90.4 us -> 80.7 us
  local copies, waits for them, and re-layouts: 12.1 us -> 7.07 us
    pallas_call x1, Pallas kernels: 90.4 us -> 80.7 us  [local(): pl.pallas_call(kernel, out_shape=(jax.ShapeDtypeStruct((rows_count, col_c...]
    pallas_call x2 -> x0, local copies, waits for them, and re-layouts: 2.79 us -> none  [local(): pl.pallas_call(kernel, out_shape=(jax.ShapeDtypeStruct((rows_count, col_c...]
    unnamed x10 -> x13, local copies, waits for them, and re-layouts: 9.31 us -> 7.07 us
    reduce_sum x1, other arithmetic: 0.22 us -> 1.36 us  [local(): table = jnp.sum(jnp.where(found, packed[None, :], 0), axis=1)]
where the time goes in v2:
time: 90 us; the launch traced here: 89.9 us
  Pallas kernels  80.7 us (90%)
  local copies, waits for them, and re-layouts  7.07 us (8%)
  other arithmetic  1.39 us (2%)
    pallas_call x1, Pallas kernels, local(): pl.pallas_call(kernel, out_shape=(jax.ShapeDtypeStruct((rows_count, col_c...  80.7 us
    unnamed x13, local copies, waits for them, and re-layouts  7.07 us

profile of v2, /device:TPU:1, one launch (start us, length us, event | category | flops | bytes accessed | tf_op | source)
XLA Modules:
  0.0 89.9 jit_solution(13293025888541717560)
XLA Ops:
  0.7 1.4 %select_reduce_fusion.table_ref = s32[256]{0:T(256)} fusion(s32[256]{0:T(256)S(1)} %fusion.3, s32[256]{0:T(256)} %plan_ref.1), kind=kLoop, calls=%fused_computation | loop fusion | flops 196352 | bytes 3072 | tf_op jit(solution)/shard_map/reduce_sum | solution.py:443
  2.0 80.7 %shard_map.110 = (bf16[256,8192]{1,0:T(8,128)(2,1)}, bf16[64,512]{1,0:T(8,128)(2,1)}, f32[2,64]{1,0:T(2,128)}, bf16[64,512]{1,0:T(8,128)(2,1)}, f32[2,64]{1,0:T(2,128)}) custom-call(s32[256]{0:T(256)} %plan_ref.1, s32[256]{0:T(256)} %select_reduce_fusion.table_ref, bf16[1,256,8192]{2,1,0:T(8,128)(2,1)} %grad_hbm.1, bf16[256,512]{1,0:T(8,128)(2,1)} %proj_ref.1, ...), custom_call_target="tpu_custom_call" | custom-call | tf_op jit(solution)/shard_map/pallas_call | solution.py:452
  82.7 0.0 copy-start.1
  82.8 0.0 copy-start.3
  82.8 0.0 copy-start
  82.8 0.0 copy-start.2
  82.8 4.7 %copy.17 = bf16[256,8192]{1,0:T(8,128)(2,1)} copy(bf16[256,8192]{1,0:T(8,128)(2,1)} %get-tuple-element.20) | data formatting | bytes 8388608
  87.5 0.0 copy-done.1
  87.5 0.6 copy.18
  88.1 0.0 copy-done.3
  88.1 0.6 copy.19
  88.7 0.0 copy-done
  88.7 0.6 copy.20
  89.3 0.0 copy-done.2
  89.3 0.6 copy.21
  (1 shorter events, 0.0 us)
Async XLA Ops:
  82.7 4.7 %copy-start.1 = (bf16[64,512]{1,0:T(8,128)(2,1)S(1)}, bf16[64,512]{1,0:T(8,128)(2,1)}, u32[]{:S(2)}) copy-start(bf16[64,512]{1,0:T(8,128)(2,1)} %get-tuple-element.21) | copy-start | bytes 196612
  82.8 5.3 %copy-start.3 = (f32[2,64]{1,0:T(2,128)S(1)}, f32[2,64]{1,0:T(2,128)}, u32[]{:S(2)}) copy-start(f32[2,64]{1,0:T(2,128)} %get-tuple-element.12) | copy-start | bytes 1540
  82.8 5.9 %copy-start = (bf16[64,512]{1,0:T(8,128)(2,1)S(1)}, bf16[64,512]{1,0:T(8,128)(2,1)}, u32[]{:S(2)}) copy-start(bf16[64,512]{1,0:T(8,128)(2,1)} %get-tuple-element.23) | copy-start | bytes 196612
  82.8 6.5 %copy-start.2 = (f32[2,64]{1,0:T(2,128)S(1)}, f32[2,64]{1,0:T(2,128)}, u32[]{:S(2)}) copy-start(f32[2,64]{1,0:T(2,128)} %get-tuple-element.14) | copy-start | bytes 1540

commit v3 on v0

v3 whole, which is shorter than its diff:
```python
import functools

import jax
import jax.numpy as jnp
from jax import lax
from jax.experimental import pallas as pl
from jax.experimental.pallas import tpu as pltpu
from jax.sharding import PartitionSpec as P

PW = 32
QB = 256
STEP = 2
RING = 4
LANES = 128

beta_one = 0.9
beta_two = 0.999
adam_eps = 1e-08
scale_eps = 1e-06

MESH = pl.DeviceIdType.MESH

CHIPS = RING**3
OWNED = 64
RANK = 512
HALF_ROWS = 256 * CHIPS
ORDERS = (("x", "y", "z"), ("y", "z", "x"), ("z", "x", "y"))
LANES_OF = (((0, 3), (1,), (2,)), ((0,), (1, 3), (2,)))
BOTH = [(half, part) for half in range(2) for part in range(3)]


def part_of(half, part):
    sizes = [PW * len(lanes) for lanes in LANES_OF[half]]
    return ORDERS[part], sizes[part], half * HALF_ROWS // 2 + sum(sizes[:part]) * CHIPS


def block_row(half, part, chip):
    order, size, base = part_of(half, part)
    a, b, c = (chip[name] for name in order)
    return base + ((a * RING + b) * RING + c) * size


def shifted(chip, axis, step):
    moved = dict(chip)
    moved[axis] = lax.rem(chip[axis] + step, RING)
    return moved


def device_of(chip, core):
    return (chip["x"], (chip["z"] * RING + chip["y"]) * 2 + core)


def rows(start, size):
    return pl.ds(pl.multiple_of(start, 32), size)


def lanes_at(block):
    return slice(block * LANES, (block + 1) * LANES)


def kernel(
    plan_ref, grad_hbm, proj_hbm, fc_hbm, fs_hbm, sc_hbm, ss_hbm,
    whole, ofc_ref, ofs_ref, osc_ref, oss_ref,
    proj_ref, fc_ref, fs_ref, sc_ref, ss_ref, grad_ref, turned, other_out, other_in, own_rows, proj_other,
    sums1, transit, recv1, sums2, recv2, sums3, recv3,
    grad_sem, small_sem, pair_send, pair_recv, first_send, first_recv, rs_send, rs_recv, near_send, near_recv, ag_send, ag_recv, fwd_send, fwd_recv,
):
    replica = lax.axis_index("replica")
    inner = lax.axis_index("fsdp")
    chip = {"x": replica, "z": inner // 8, "y": lax.rem(inner // 2, RING)}
    core = lax.rem(inner, 2)
    other = 1 - core
    sibling = device_of(chip, other)
    cols = grad_hbm.shape[2] // RING

    loads = []
    for j in range(RING):
        loads.append(
            pltpu.make_async_copy(
                grad_hbm.at[0, :, pl.ds(j * cols, cols)], grad_ref.at[:, pl.ds(j * cols, cols)], grad_sem.at[j]
            )
        )
        loads[-1].start()

    small = []
    for i, (source, target) in enumerate(
        ((proj_hbm, proj_ref), (fc_hbm, fc_ref), (fs_hbm, fs_ref), (sc_hbm, sc_ref), (ss_hbm, ss_ref))
    ):
        small.append(pltpu.make_async_copy(source, target, small_sem.at[i]))
        small[-1].start()

    barrier = pltpu.get_barrier_semaphore()
    pl.semaphore_signal(barrier, inc=1, device_id=sibling, device_id_type=MESH)
    for axis in ("x", "y", "z"):
        for step in range(1, RING):
            pl.semaphore_signal(
                barrier, inc=1, device_id=device_of(shifted(chip, axis, step), core), device_id_type=MESH
            )

    for j in range(RING):
        loads[j].wait()

        @pl.loop(0, cols // 256)
        def _(t, j=j):
            at = pl.multiple_of(j * cols + t * 256, 256)
            block = grad_ref[:, pl.ds(at, 256)].T
            turned[pl.ds(at // PW, 256 // PW)] = block.reshape(256 // PW, PW, block.shape[1])

    for copy in small:
        copy.wait()
    pl.semaphore_wait(barrier, 3 * (RING - 1) + 1)

    def remote(src, dst, send, recv, target):
        return pltpu.make_async_remote_copy(
            src_ref=src, dst_ref=dst, send_sem=send, recv_sem=recv, device_id=target, device_id_type=MESH
        )

    proj_copy = remote(proj_ref, proj_other, pair_send.at[2], pair_recv.at[2], sibling)
    proj_copy.start()

    span = CHIPS * PW

    def pick(target, which, half):
        @pl.loop(0, CHIPS)
        def _(t):
            target[rows(half * span + t * PW, PW), :] = turned[plan_ref[(t * 2 + which) * 2 + half]]

    pair = []
    for half in range(2):
        pick(other_out, other, half)
        part_rows = pl.ds(half * span, span)
        pair.append(
            remote(
                other_out.at[part_rows, :], other_in.at[part_rows, :],
                pair_send.at[half], pair_recv.at[half], sibling,
            )
        )
        pair[-1].start()

    def project(half):
        pick(own_rows, core, half)
        if half == 0:
            proj_copy.wait_recv()
        pair[half].wait_recv()

        @pl.loop(0, CHIPS // 8)
        def _(t):
            at = rows(half * span + t * 8 * PW, 8 * PW)
            product = jnp.dot(own_rows[at, :], proj_ref[...], preferred_element_type=jnp.float32)
            product += jnp.dot(other_in[at, :], proj_other[...], preferred_element_type=jnp.float32)
            for i in range(8):
                to = {"x": t // 2, "z": (t % 2) * 2 + i // 4, "y": i % 4}
                for part in range(3):
                    for j, block in enumerate(LANES_OF[half][part]):
                        sums1[rows(block_row(half, part, to) + j * PW, PW), :] = product[
                            i * PW : (i + 1) * PW, lanes_at(block)
                        ].astype(jnp.bfloat16)

    def sub_row(half, part, a, b):
        order = ORDERS[part]
        return block_row(half, part, {order[0]: a, order[1]: b, order[2]: 0})

    opening, middle, closing = {}, {}, {}
    for half, part in BOTH:
        order, size, base = part_of(half, part)
        a = chip[order[0]]
        message = 2 * size * RING
        for way, flow in enumerate((1, RING - 1)):
            onward = device_of(shifted(chip, order[0], flow), core)
            backward = device_of(shifted(chip, order[0], RING - flow), core)
            sem = half * 6 + part * 2 + way
            land = base // 2 + way * 2 * message
            for kind, (steps, landing, place, target) in enumerate(
                (
                    (2, transit, base // 4 + way * message, onward),
                    (RING - flow, recv1, land, backward),
                    (flow, recv1, land + message, onward),
                )
            ):
                opening[kind, half, part, way] = remote(
                    sums1.at[rows(sub_row(half, part, lax.rem(a + steps, RING), 2 * way), message), :],
                    landing.at[pl.ds(place, message), :],
                    first_send.at[12 * kind + sem], first_recv.at[12 * kind + sem], target,
                )
        for stage, source, landing, copies in ((1, sums2, recv2, middle), (2, sums3, recv3, closing)):
            unit = size * RING ** (2 - stage)
            origin = base // RING**stage
            for step in range(1, RING):
                to = shifted(chip, order[stage], step)
                sem = (stage - 1) * 18 + half * 9 + part * 3 + step - 1
                copies[half, part, step] = remote(
                    source.at[rows(origin + to[order[stage]] * unit, unit), :],
                    landing.at[pl.ds(3 * base // RING ** (stage + 1) + (step - 1) * unit, unit), :],
                    rs_send.at[sem], rs_recv.at[sem], device_of(to, core),
                )

    def opening_start(kind, half):
        for part in range(3):
            for way in range(2):
                opening[kind, half, part, way].start()

    def add(count, target, at, *terms):
        tile = 128

        @pl.loop(0, count // tile)
        def _(t):
            total = sum(ref[rows(row + t * tile, tile), :].astype(jnp.float32) for ref, row in terms)
            target[rows(at + t * tile, tile), :] = total.astype(jnp.bfloat16)

    def pass_on(half):
        for part in range(3):
            order, size, base = part_of(half, part)
            message = 2 * size * RING
            for way, flow in enumerate((1, RING - 1)):
                opening[0, half, part, way].wait_recv()
                own = sub_row(half, part, lax.rem(chip[order[0]] + flow, RING), 2 * way)
                add(message, sums1, own, (sums1, own), (transit, base // 4 + way * message))
                opening[2, half, part, way].start()

    def first_done(half):
        for part in range(3):
            order, size, base = part_of(half, part)
            message = 2 * size * RING
            for way in range(2):
                opening[1, half, part, way].wait_recv()
                opening[2, half, part, way].wait_recv()
                own = sub_row(half, part, chip[order[0]], 2 * way)
                land = base // 2 + way * 2 * message
                add(
                    message, sums2, base // RING + way * message,
                    (sums1, own), (recv1, land), (recv1, land + message),
                )
            for step in (2, 1, 3):
                middle[half, part, step].start()

    def middle_done(half):
        for part in range(3):
            order, size, base = part_of(half, part)
            for step in range(1, RING):
                middle[half, part, step].wait_recv()
            unit = size * RING
            own = base // RING + chip[order[1]] * unit
            landings = [(recv2, 3 * base // RING**2 + i * unit) for i in range(3)]
            add(unit, sums3, base // RING**2, (sums2, own), *landings)
            for step in (2, 1, 3):
                closing[half, part, step].start()

    first_scales, second_scales = fs_ref[...].T, ss_ref[...].T
    peaks = ([], [])

    def adam(half):
        low = {}
        for part in range(3):
            order, size, base = part_of(half, part)
            for step in range(1, RING):
                closing[half, part, step].wait_recv()
            total = sums3[rows(base // 16 + chip[order[2]] * size, size), :].astype(jnp.float32)
            for i in range(3):
                total += recv3[pl.ds(3 * base // 64 + i * size, size), :].astype(jnp.float32)
            for j, block in enumerate(LANES_OF[half][part]):
                low[block] = total[j * PW : (j + 1) * PW, :]
        row = slice(half * PW, (half + 1) * PW)
        mine_peaks = ([], [])
        direction = {}
        for b in range(RANK // QB):
            lane = slice(b * QB, (b + 1) * QB)
            lowrank = jnp.concatenate([low[2 * b], low[2 * b + 1]], axis=1)
            first = fc_ref[row, lane].astype(jnp.float32) * first_scales[row, b : b + 1]
            second = sc_ref[row, lane].astype(jnp.float32) * second_scales[row, b : b + 1]
            first_new = beta_one * first + (1.0 - beta_one) * lowrank
            second_new = beta_two * second + (1.0 - beta_two) * lowrank * lowrank
            corr_one = 1.0 - beta_one**STEP
            corr_two = 1.0 - beta_two**STEP
            result = (first_new / corr_one / (jnp.sqrt(second_new / corr_two) + adam_eps)).astype(jnp.bfloat16)
            for i in range(2):
                direction[2 * b + i] = result[:, lanes_at(i)]
            for i, (value, codes) in enumerate(((first_new, ofc_ref), (second_new, osc_ref))):
                peak = jnp.max(jnp.abs(value), axis=1, keepdims=True) + scale_eps
                codes[row, lane] = (value / peak).astype(jnp.bfloat16)
                mine_peaks[i].append(peak)
        for i in range(2):
            peaks[i].append(jnp.concatenate(mine_peaks[i], axis=1))
        for part in range(3):
            at = (mine + block_row(half, part, chip)) // PW
            for j, block in enumerate(LANES_OF[half][part]):
                whole[at + j] = direction[block]

    mine, theirs = core * HALF_ROWS, other * HALF_ROWS
    started, forwards = [], []

    def copy_of(start, size, send, recv, target):
        where = whole.at[pl.ds(start // PW, size // PW)]
        return remote(where, where, send, recv, target)

    def spread(start, size, send, recv, target):
        started.append(copy_of(mine + start, size, send, recv, target))
        started[-1].start()

    def forward(start, size):
        index = len(forwards)
        forwards.append((start, size))
        spread(start, size, fwd_send.at[index], fwd_recv.at[index], sibling)

    def landed(start, size, recv):
        copy_of(mine + start, size, first_send.at[0], recv, sibling).wait_recv()
        return start, size

    def direct_start(stage, half):
        for part in range(3):
            order, size, base = part_of(half, part)
            if stage == 2:
                piece = block_row(half, part, chip), size
            else:
                for step in range(1, RING):
                    start = block_row(half, part, shifted(chip, order[2], RING - step))
                    landed(start, size, ag_recv.at[18 + half * 9 + part * 3 + step - 1])
                piece = sub_row(half, part, chip[order[0]], chip[order[1]]), size * RING
            for step in (2, 1, 3):
                sem = (stage - 1) * 18 + half * 9 + part * 3 + step - 1
                to = device_of(shifted(chip, order[stage], step), core)
                spread(*piece, ag_send.at[sem], ag_recv.at[sem], to)

    def wide_piece(half, part, a_off, way):
        order, size, base = part_of(half, part)
        return sub_row(half, part, lax.rem(chip[order[0]] + a_off, RING), 2 * way), 2 * size * RING

    def near_start(half):
        for part in range(3):
            order, size, base = part_of(half, part)
            for step in range(1, RING):
                start = sub_row(half, part, chip[order[0]], lax.rem(chip[order[1]] + RING - step, RING))
                landed(start, size * RING, ag_recv.at[half * 9 + part * 3 + step - 1])
            for turn in range(2):
                for way, flow in enumerate((1, RING - 1)):
                    content = way ^ turn
                    sem = half * 12 + part * 4 + way * 2 + content
                    to = device_of(shifted(chip, order[0], flow), core)
                    spread(*wide_piece(half, part, 0, content), near_send.at[sem], near_recv.at[sem], to)
            forward(sub_row(half, part, chip[order[0]], 0), size * RING * RING)

    def near_landed(half, turn):
        for part in range(3):
            order = ORDERS[part]
            for way, flow in enumerate((1, RING - 1)):
                content = way ^ turn
                piece = landed(
                    *wide_piece(half, part, RING - flow, content),
                    near_recv.at[half * 12 + part * 4 + way * 2 + content],
                )
                if turn == 0:
                    sem = 24 + half * 6 + part * 2 + way
                    to = device_of(shifted(chip, order[0], flow), core)
                    spread(*piece, near_send.at[sem], near_recv.at[sem], to)
                forward(*piece)

    def far_landed(half):
        for part in range(3):
            for way in range(2):
                forward(*landed(*wide_piece(half, part, 2, way), near_recv.at[24 + half * 6 + part * 2 + way]))

    project(0)
    opening_start(0, 0)
    opening_start(1, 0)
    project(1)
    opening_start(0, 1)
    pass_on(0)
    opening_start(1, 1)
    pass_on(1)
    first_done(0)
    middle_done(0)
    first_done(1)
    adam(0)
    direct_start(2, 0)
    middle_done(1)
    direct_start(1, 0)
    adam(1)
    direct_start(2, 1)
    near_start(0)
    direct_start(1, 1)
    near_start(1)
    for turn in range(2):
        for half in range(2):
            near_landed(half, turn)
    far_landed(0)
    far_landed(1)
    ofs_ref[...] = jnp.concatenate(peaks[0], axis=0).T
    oss_ref[...] = jnp.concatenate(peaks[1], axis=0).T
    for index, (start, size) in enumerate(forwards):
        copy_of(theirs + start, size, first_send.at[0], fwd_recv.at[index], sibling).wait_recv()

    proj_copy.wait_send()
    for copy in pair:
        copy.wait_send()
    for stage in (opening, middle, closing):
        for copy in stage.values():
            copy.wait_send()
    for copy in started:
        copy.wait_send()


def finish(table_ref, whole, proj_hbm, *refs):
    passed, update_hbm, outs = refs[:4], refs[4], refs[5:9]
    proj_ref, natural, update_ref, out_sem, pass_sem, proj_sem = refs[9:]
    load = pltpu.make_async_copy(proj_hbm, proj_ref, proj_sem)
    load.start()
    passing = [pltpu.make_async_copy(passed[i], outs[i], pass_sem.at[i]) for i in range(4)]
    for copy in passing:
        copy.start()
    tile = natural.shape[0]
    steps = update_ref.shape[1] // tile
    stores = []
    for t in range(steps):
        cols = pl.ds(t * tile, tile)
        stores.append(pltpu.make_async_copy(update_ref.at[:, cols], update_hbm.at[:, cols], out_sem.at[t]))

    load.wait()

    @pl.loop(0, steps)
    def _(t):
        for p in range(tile // PW):
            packed = table_ref[t * (tile // PW) + p]
            half = lax.shift_right_logical(packed, 30)
            starts = [lax.shift_right_logical(packed, 10 * part) & 1023 for part in range(3)]
            sources = starts + [starts[0] + 1 + half * (starts[1] - starts[0])]
            for lane, source in enumerate(sources):
                natural[p * PW : (p + 1) * PW, lanes_at(lane)] = whole[source]
        product = lax.dot_general(
            proj_ref[...], natural[...], (((1,), (1,)), ((), ())), preferred_element_type=jnp.float32
        )
        cols = pl.ds(pl.multiple_of(t * tile, tile), tile)
        update_ref[:, cols] = product.astype(jnp.bfloat16)
        pltpu.make_async_copy(update_ref.at[:, cols], update_hbm.at[:, cols], out_sem.at[t]).start()

    for copy in stores + passing:
        copy.wait()


def in_hbm(array):
    return pltpu.with_memory_space_constraint(array, pltpu.HBM)


def local(gradients, projection, plan, first_codes, first_scales, second_codes, second_scales):
    panel_count = plan.shape[0]
    position = jnp.arange(panel_count, dtype=jnp.int32)
    owner = position // 2
    half = position % 2
    chip = {"x": owner // 32, "z": owner // 8 % RING, "y": owner // 2 % RING}
    base = (owner % 2) * HALF_ROWS
    starts = [
        (base + jnp.where(half == 0, block_row(0, part, chip), block_row(1, part, chip))) // PW for part in range(3)
    ]
    packed = starts[0] + starts[1] * 1024 + starts[2] * 1024 * 1024 + half * 1024 * 1024 * 1024
    found = plan[None, :] == position[:, None]
    table = jnp.sum(jnp.where(found, packed[None, :], 0), axis=1)

    bf16, f32 = jnp.bfloat16, jnp.float32
    vmem = pl.BlockSpec(memory_space=pltpu.VMEM)
    smem = pl.BlockSpec(memory_space=pltpu.SMEM)
    hbm = pl.BlockSpec(memory_space=pltpu.HBM)
    sem = pltpu.SemaphoreType.DMA
    rows_count, col_count = gradients.shape[1:]
    half_cols = col_count // 2
    whole, *moments = pl.pallas_call(
        kernel,
        out_shape=(
            pltpu.VMEM((2 * HALF_ROWS // PW, PW, LANES), bf16),
            jax.ShapeDtypeStruct(first_codes.shape, bf16),
            jax.ShapeDtypeStruct(first_scales.shape[::-1], f32),
            jax.ShapeDtypeStruct(second_codes.shape, bf16),
            jax.ShapeDtypeStruct(second_scales.shape[::-1], f32),
        ),
        in_specs=[smem] + [hbm] * 6,
        out_specs=(vmem, vmem, vmem, vmem, vmem),
        scratch_shapes=[
            pltpu.VMEM(projection.shape, bf16),
            pltpu.VMEM(first_codes.shape, bf16),
            pltpu.VMEM(first_scales.shape[::-1], f32),
            pltpu.VMEM(second_codes.shape, bf16),
            pltpu.VMEM(second_scales.shape[::-1], f32),
            pltpu.VMEM((rows_count, col_count), bf16),
            pltpu.VMEM((col_count // PW, PW, rows_count), bf16),
            pltpu.VMEM((half_cols, rows_count), bf16),
            pltpu.VMEM((half_cols, rows_count), bf16),
            pltpu.VMEM((half_cols, rows_count), bf16),
            pltpu.VMEM(projection.shape, bf16),
            pltpu.VMEM((HALF_ROWS, LANES), bf16),
            pltpu.VMEM((HALF_ROWS // 4, LANES), bf16),
            pltpu.VMEM((HALF_ROWS // 2, LANES), bf16),
            pltpu.VMEM((HALF_ROWS // 4, LANES), bf16),
            pltpu.VMEM((HALF_ROWS * 3 // 16, LANES), bf16),
            pltpu.VMEM((HALF_ROWS // 16, LANES), bf16),
            pltpu.VMEM((HALF_ROWS * 3 // 64, LANES), bf16),
            sem((4,)), sem((5,)), sem((3,)), sem((3,)), sem((36,)), sem((36,)), sem((36,)), sem((36,)), sem((36,)), sem((36,)),
            sem((36,)), sem((36,)), sem((42,)), sem((42,)),
        ],
        compiler_params=pltpu.CompilerParams(
            collective_id=0, has_side_effects=True, vmem_limit_bytes=54 * 1024 * 1024
        ),
    )(plan, *map(in_hbm, (gradients, projection, first_codes, first_scales.T, second_codes, second_scales.T)))
    update, first_out, first_peak, second_out, second_peak = pl.pallas_call(
        finish,
        out_shape=[jax.ShapeDtypeStruct((rows_count, col_count), bf16)]
        + [jax.ShapeDtypeStruct(moment.shape, moment.dtype) for moment in moments],
        in_specs=[smem, vmem] + [hbm] * 5,
        out_specs=[hbm] * 5,
        scratch_shapes=[
            pltpu.VMEM(projection.shape, bf16),
            pltpu.VMEM((512, RANK), bf16),
            pltpu.VMEM((rows_count, col_count), bf16),
            sem((col_count // 512,)),
            sem((4,)),
            sem,
        ],
        compiler_params=pltpu.CompilerParams(vmem_limit_bytes=24 * 1024 * 1024),
    )(table, pltpu.with_memory_space_constraint(whole, pltpu.VMEM), in_hbm(projection), *map(in_hbm, moments))
    return update, first_out, first_peak.T, second_out, second_peak.T


def solution(mesh):
    in_specs = (
        P("replica", "fsdp", None),
        P("fsdp", None),
        P(),
        P(("replica", "fsdp"), None),
        P(("replica", "fsdp"), None),
        P(("replica", "fsdp"), None),
        P(("replica", "fsdp"), None),
    )
    out_specs = (
        P("fsdp", None),
        P(("replica", "fsdp"), None),
        P(("replica", "fsdp"), None),
        P(("replica", "fsdp"), None),
        P(("replica", "fsdp"), None),
    )
    return jax.shard_map(local, mesh=mesh, in_specs=in_specs, out_specs=out_specs, check_vma=False)
```

time: 197 us -> 79.1 us (0.40)
  waiting for transfers between devices: 107 us -> 0 us
  Pallas kernels: 0 us -> 77.5 us
  local copies, waits for them, and re-layouts: 27.1 us -> 0 us
  blocking collectives: 21 us -> 0 us
  between operations: 15.7 us -> 0.65 us
  other arithmetic: 10.4 us -> 0.83 us
  starting transfers between devices: 7.77 us -> 0 us
  matrix products: 7.74 us -> 0 us
    pallas_call x0 -> x2, Pallas kernels: none -> 77.5 us  [the longest x1 68.9 us: local(): pl.pallas_call(kernel, out_shape=(pltpu.VMEM((2 * HALF_ROWS // PW, PW, LA...]
    reduce_scatter x1 -> x0, waiting for transfers between devices: 49.6 us -> none  [local(): lax.psum_scatter(reordered, 'replica', scatter_dimension=1, tiled=True)]
    all_gather x2 -> x0, waiting for transfers between devices: 39.9 us -> none  [the longest x1 39.9 us: local(): ordered = lax.all_gather(returned, 'replica', axis=1, tiled=True)]
    all_to_all x1 -> x0, blocking collectives: 21 us -> none  [local(): lax.all_to_all(owner_block, 'fsdp', split_axis=0, concat_axis=1, tiled=True)]
    all_to_all x1 -> x0, waiting for transfers between devices: 16.6 us -> none  [local(): lax.all_to_all(summed.astype(jnp.bfloat16), 'fsdp', split_axis=1, concat_...]
    unnamed x20 -> x0, local copies, waits for them, and re-layouts: 14.8 us -> none
    gather x2 -> x0, local copies, waits for them, and re-layouts: 9.97 us -> none  [the longest x1 5.02 us: local(): jnp.take(ordered.reshape(row_count, panel_count, PW), inverse, axis=1)]
    select_n x4 -> x0, other arithmetic: 8.73 us -> none  [the longest x1 4.06 us: local(): reordered = jnp.take(grad_local, plan, axis=1).reshape(row_count, col_count)]
  transfers between devices with their start and end apart: 4 -> 0, of which waited for: 3 -> 0; matrix products, arithmetic and copies ran while one was open for 2% -> 0% of each run, Pallas kernels for 0% -> 0%
where the time goes in v3:
time: 79.1 us; the launch traced here: 79 us
  Pallas kernels  77.5 us (98%)
  other arithmetic  0.83 us (1%)
    pallas_call x1, Pallas kernels, local(): pl.pallas_call(kernel, out_shape=(pltpu.VMEM((2 * HALF_ROWS // PW, PW, LA...  68.9 us
    pallas_call x1, Pallas kernels, local(): pl.pallas_call(finish, out_shape=[jax.ShapeDtypeStruct((rows_count, col_c...  8.61 us

profile of v3, /device:TPU:1, one launch (start us, length us, event | category | flops | bytes accessed | tf_op | source)
XLA Modules:
  0.0 79.0 jit_solution(5768582488559114284)
XLA Ops:
  0.7 0.8 %select_reduce_fusion.table_ref = s32[256]{0:T(256)S(1)} fusion(s32[256]{0:T(256)S(1)} %multiply_add_fusion, s32[256]{0:T(256)} %plan_ref.1), kind=kLoop, calls=%fused_computation | loop fusion | flops 196352 | bytes 3072 | tf_op jit(solution)/shard_map/reduce_sum | solution.py:454
  1.5 68.9 %shard_map.110 = (bf16[1024,32,128]{2,1,0:T(8,128)(2,1)S(1)}, bf16[64,512]{1,0:T(8,128)(2,1)}, f32[2,64]{1,0:T(2,128)}, bf16[64,512]{1,0:T(8,128)(2,1)}, f32[2,64]{1,0:T(2,128)}) custom-call(s32[256]{0:T(256)} %plan_ref.1, bf16[1,256,8192]{2,1,0:T(8,128)(2,1)} %grad_hbm.1, bf16[256,512]{1,0:T(8,128)(2,1)} %proj_hbm.3, bf16[64,512]{1,0:T(8,128)(2,1)} %fc_hbm.1, ...), custom_call_target="tpu_custom_call" | custom-call | tf_op jit(solution)/shard_map/pallas_call | solution.py:463
  70.3 8.6 %shard_map.111 = (bf16[256,8192]{1,0:T(8,128)(2,1)}, bf16[64,512]{1,0:T(8,128)(2,1)}, f32[2,64]{1,0:T(2,128)}, bf16[64,512]{1,0:T(8,128)(2,1)}, f32[2,64]{1,0:T(2,128)}) custom-call(s32[256]{0:T(256)S(1)} %select_reduce_fusion.table_ref, bf16[1024,32,128]{2,1,0:T(8,128)(2,1)S(1)} %get-tuple-element.15.whole, bf16[256,512]{1,0:T(8,128)(2,1)} %proj_hbm.3, ...), custom_call_target="tpu_custom_call" | custom-call | tf_op jit(solution)/shard_map/pallas_call | solution.py:500
  (1 shorter events, 0.0 us)

commit v4 on v3

--- a/solution.py
+++ b/solution.py
@@ -417,15 +417,16 @@
 
     @pl.loop(0, steps)
     def _(t):
+        pieces = []
         for p in range(tile // PW):
             packed = table_ref[t * (tile // PW) + p]
             half = lax.shift_right_logical(packed, 30)
             starts = [lax.shift_right_logical(packed, 10 * part) & 1023 for part in range(3)]
             sources = starts + [starts[0] + 1 + half * (starts[1] - starts[0])]
-            for lane, source in enumerate(sources):
-                natural[p * PW : (p + 1) * PW, lanes_at(lane)] = whole[source]
+            pieces.append(jnp.concatenate([whole[source] for source in sources], axis=1))
+        picked = jnp.concatenate(pieces, axis=0)
         product = lax.dot_general(
-            proj_ref[...], natural[...], (((1,), (1,)), ((), ())), preferred_element_type=jnp.float32
+            proj_ref[...], picked, (((1,), (1,)), ((), ())), preferred_element_type=jnp.float32
         )
         cols = pl.ds(pl.multiple_of(t * tile, tile), tile)
         update_ref[:, cols] = product.astype(jnp.bfloat16)
@@ -505,9 +506,9 @@
         out_specs=[hbm] * 5,
         scratch_shapes=[
             pltpu.VMEM(projection.shape, bf16),
-            pltpu.VMEM((512, RANK), bf16),
+            pltpu.VMEM((2048, RANK), bf16),
             pltpu.VMEM((rows_count, col_count), bf16),
-            sem((col_count // 512,)),
+            sem((col_count // 2048,)),
             sem((4,)),
             sem,
         ],

time: 79.1 us -> 76.4 us (0.966)
  Pallas kernels: 77.5 us -> 74.8 us
    pallas_call x1, Pallas kernels: 8.61 us -> 5.92 us  [local(): pl.pallas_call(finish, out_shape=[jax.ShapeDtypeStruct((rows_count, col_c...]
where the time goes in v4:
time: 76.4 us; the launch traced here: 76.3 us
  Pallas kernels  74.8 us (98%)
  other arithmetic  0.83 us (1%)
    pallas_call x1, Pallas kernels, local(): pl.pallas_call(kernel, out_shape=(pltpu.VMEM((2 * HALF_ROWS // PW, PW, LA...  68.9 us
    pallas_call x1, Pallas kernels, local(): pl.pallas_call(finish, out_shape=[jax.ShapeDtypeStruct((rows_count, col_c...  5.92 us

profile of v4, /device:TPU:1, one launch (start us, length us, event | category | flops | bytes accessed | tf_op | source)
XLA Modules:
  0.0 76.3 jit_solution(16039215843801899822)
XLA Ops:
  0.7 0.8 %select_reduce_fusion.table_ref = s32[256]{0:T(256)S(1)} fusion(s32[256]{0:T(256)S(1)} %multiply_add_fusion, s32[256]{0:T(256)} %plan_ref.1), kind=kLoop, calls=%fused_computation | loop fusion | flops 196352 | bytes 3072 | tf_op jit(solution)/shard_map/reduce_sum | solution.py:455
  1.5 68.9 %shard_map.110 = (bf16[1024,32,128]{2,1,0:T(8,128)(2,1)S(1)}, bf16[64,512]{1,0:T(8,128)(2,1)}, f32[2,64]{1,0:T(2,128)}, bf16[64,512]{1,0:T(8,128)(2,1)}, f32[2,64]{1,0:T(2,128)}) custom-call(s32[256]{0:T(256)} %plan_ref.1, bf16[1,256,8192]{2,1,0:T(8,128)(2,1)} %grad_hbm.1, bf16[256,512]{1,0:T(8,128)(2,1)} %proj_hbm.3, bf16[64,512]{1,0:T(8,128)(2,1)} %fc_hbm.1, ...), custom_call_target="tpu_custom_call" | custom-call | tf_op jit(solution)/shard_map/pallas_call | solution.py:464
  70.3 5.9 %shard_map.111 = (bf16[256,8192]{1,0:T(8,128)(2,1)}, bf16[64,512]{1,0:T(8,128)(2,1)}, f32[2,64]{1,0:T(2,128)}, bf16[64,512]{1,0:T(8,128)(2,1)}, f32[2,64]{1,0:T(2,128)}) custom-call(s32[256]{0:T(256)S(1)} %select_reduce_fusion.table_ref, bf16[1024,32,128]{2,1,0:T(8,128)(2,1)S(1)} %get-tuple-element.15.whole, bf16[256,512]{1,0:T(8,128)(2,1)} %proj_hbm.3, ...), custom_call_target="tpu_custom_call" | custom-call | tf_op jit(solution)/shard_map/pallas_call | solution.py:501
  (1 shorter events, 0.0 us)

commit v5 on v4

--- a/solution.py
+++ b/solution.py
@@ -367,8 +367,8 @@
     opening_start(1, 1)
     pass_on(1)
     first_done(0)
+    first_done(1)
     middle_done(0)
-    first_done(1)
     adam(0)
     direct_start(2, 0)
     middle_done(1)
@@ -440,6 +440,10 @@
     return pltpu.with_memory_space_constraint(array, pltpu.HBM)
 
 
+def in_vmem(array):
+    return pltpu.with_memory_space_constraint(array, pltpu.VMEM)
+
+
 def local(gradients, projection, plan, first_codes, first_scales, second_codes, second_scales):
     panel_count = plan.shape[0]
     position = jnp.arange(panel_count, dtype=jnp.int32)
@@ -465,10 +469,10 @@
         kernel,
         out_shape=(
             pltpu.VMEM((2 * HALF_ROWS // PW, PW, LANES), bf16),
-            jax.ShapeDtypeStruct(first_codes.shape, bf16),
-            jax.ShapeDtypeStruct(first_scales.shape[::-1], f32),
-            jax.ShapeDtypeStruct(second_codes.shape, bf16),
-            jax.ShapeDtypeStruct(second_scales.shape[::-1], f32),
+            pltpu.VMEM((first_codes.shape), bf16),
+            pltpu.VMEM((first_scales.shape[::-1]), f32),
+            pltpu.VMEM((second_codes.shape), bf16),
+            pltpu.VMEM((second_scales.shape[::-1]), f32),
         ),
         in_specs=[smem] + [hbm] * 6,
         out_specs=(vmem, vmem, vmem, vmem, vmem),
@@ -502,7 +506,7 @@
         finish,
         out_shape=[jax.ShapeDtypeStruct((rows_count, col_count), bf16)]
         + [jax.ShapeDtypeStruct(moment.shape, moment.dtype) for moment in moments],
-        in_specs=[smem, vmem] + [hbm] * 5,
+        in_specs=[smem, vmem, hbm] + [vmem] * 4,
         out_specs=[hbm] * 5,
         scratch_shapes=[
             pltpu.VMEM(projection.shape, bf16),
@@ -513,7 +517,7 @@
             sem,
         ],
         compiler_params=pltpu.CompilerParams(vmem_limit_bytes=24 * 1024 * 1024),
-    )(table, pltpu.with_memory_space_constraint(whole, pltpu.VMEM), in_hbm(projection), *map(in_hbm, moments))
+    )(table, in_vmem(whole), in_hbm(projection), *map(in_vmem, moments))
     return update, first_out, first_peak.T, second_out, second_peak.T
 
 

time: 76.4 us -> 75.3 us (0.986)
  Pallas kernels: 74.8 us -> 73.6 us
    pallas_call x1, Pallas kernels: 68.9 us -> 67.7 us  [local(): pl.pallas_call(kernel, out_shape=(pltpu.VMEM((2 * HALF_ROWS // PW, PW, LA...]
where the time goes in v5:
time: 75.3 us; the launch traced here: 75.1 us
  Pallas kernels  73.6 us (98%)
  other arithmetic  0.83 us (1%)
    pallas_call x1, Pallas kernels, local(): pl.pallas_call(kernel, out_shape=(pltpu.VMEM((2 * HALF_ROWS // PW, PW, LA...  67.7 us
    pallas_call x1, Pallas kernels, local(): pl.pallas_call(finish, out_shape=[jax.ShapeDtypeStruct((rows_count, col_c...  5.96 us

profile of v5, /device:TPU:1, one launch (start us, length us, event | category | flops | bytes accessed | tf_op | source)
XLA Modules:
  0.0 75.1 jit_solution(12270936955554793196)
XLA Ops:
  0.7 0.8 %select_reduce_fusion.table_ref = s32[256]{0:T(256)S(1)} fusion(s32[256]{0:T(256)S(1)} %multiply_add_fusion, s32[256]{0:T(256)} %plan_ref.1), kind=kLoop, calls=%fused_computation | loop fusion | flops 196352 | bytes 3072 | tf_op jit(solution)/shard_map/reduce_sum | solution.py:459
  1.5 67.7 %shard_map.110 = (bf16[1024,32,128]{2,1,0:T(8,128)(2,1)S(1)}, bf16[64,512]{1,0:T(8,128)(2,1)S(1)}, f32[2,64]{1,0:T(2,128)S(1)}, bf16[64,512]{1,0:T(8,128)(2,1)S(1)}, f32[2,64]{1,0:T(2,128)S(1)}) custom-call(s32[256]{0:T(256)} %plan_ref.1, bf16[1,256,8192]{2,1,0:T(8,128)(2,1)} %grad_hbm.1, bf16[256,512]{1,0:T(8,128)(2,1)} %proj_hbm.3, ...), custom_call_target="tpu_custom_call" | custom-call | tf_op jit(solution)/shard_map/pallas_call | solution.py:468
  69.2 6.0 %shard_map.111 = (bf16[256,8192]{1,0:T(8,128)(2,1)}, bf16[64,512]{1,0:T(8,128)(2,1)}, f32[2,64]{1,0:T(2,128)}, bf16[64,512]{1,0:T(8,128)(2,1)}, f32[2,64]{1,0:T(2,128)}) custom-call(s32[256]{0:T(256)S(1)} %select_reduce_fusion.table_ref, bf16[1024,32,128]{2,1,0:T(8,128)(2,1)S(1)} %get-tuple-element.15.whole, bf16[256,512]{1,0:T(8,128)(2,1)} %proj_hbm.3, ...), custom_call_target="tpu_custom_call" | custom-call | tf_op jit(solution)/shard_map/pallas_call | solution.py:505
  (1 shorter events, 0.0 us)

commit v6 on v5

--- a/solution.py
+++ b/solution.py
@@ -398,11 +398,9 @@
         copy.wait_send()
 
 
-def finish(table_ref, whole, proj_hbm, *refs):
+def finish(table_ref, whole, proj_ref, *refs):
     passed, update_hbm, outs = refs[:4], refs[4], refs[5:9]
-    proj_ref, natural, update_ref, out_sem, pass_sem, proj_sem = refs[9:]
-    load = pltpu.make_async_copy(proj_hbm, proj_ref, proj_sem)
-    load.start()
+    natural, update_ref, out_sem, pass_sem = refs[9:]
     passing = [pltpu.make_async_copy(passed[i], outs[i], pass_sem.at[i]) for i in range(4)]
     for copy in passing:
         copy.start()
@@ -412,8 +410,6 @@
     for t in range(steps):
         cols = pl.ds(t * tile, tile)
         stores.append(pltpu.make_async_copy(update_ref.at[:, cols], update_hbm.at[:, cols], out_sem.at[t]))
-
-    load.wait()
 
     @pl.loop(0, steps)
     def _(t):
@@ -506,18 +502,16 @@
         finish,
         out_shape=[jax.ShapeDtypeStruct((rows_count, col_count), bf16)]
         + [jax.ShapeDtypeStruct(moment.shape, moment.dtype) for moment in moments],
-        in_specs=[smem, vmem, hbm] + [vmem] * 4,
+        in_specs=[smem, vmem, vmem] + [vmem] * 4,
         out_specs=[hbm] * 5,
         scratch_shapes=[
-            pltpu.VMEM(projection.shape, bf16),
             pltpu.VMEM((2048, RANK), bf16),
             pltpu.VMEM((rows_count, col_count), bf16),
             sem((col_count // 2048,)),
             sem((4,)),
-            sem,
         ],
         compiler_params=pltpu.CompilerParams(vmem_limit_bytes=24 * 1024 * 1024),
-    )(table, in_vmem(whole), in_hbm(projection), *map(in_vmem, moments))
+    )(table, in_vmem(whole), in_vmem(projection), *map(in_vmem, moments))
     return update, first_out, first_peak.T, second_out, second_peak.T
 
 

time: 75.3 us -> 74.4 us (0.988)
  Pallas kernels: 73.6 us -> 72.7 us
    pallas_call x1, Pallas kernels: 5.96 us -> 5.01 us  [local(): pl.pallas_call(finish, out_shape=[jax.ShapeDtypeStruct((rows_count, col_c...]
where the time goes in v6:
time: 74.4 us; the launch traced here: 74.2 us
  Pallas kernels  72.7 us (98%)
  other arithmetic  0.86 us (1%)
    pallas_call x1, Pallas kernels, local(): pl.pallas_call(kernel, out_shape=(pltpu.VMEM((2 * HALF_ROWS // PW, PW, LA...  67.7 us
    pallas_call x1, Pallas kernels, local(): pl.pallas_call(finish, out_shape=[jax.ShapeDtypeStruct((rows_count, col_c...  5.01 us

profile of v6, /device:TPU:1, one launch (start us, length us, event | category | flops | bytes accessed | tf_op | source)
XLA Modules:
  0.0 74.2 jit_solution(8477154332907358121)
XLA Ops:
  0.6 0.0 copy-start
  0.7 0.8 %select_reduce_fusion.table_ref = s32[256]{0:T(256)S(1)} fusion(s32[256]{0:T(256)S(1)} %multiply_add_fusion, s32[256]{0:T(256)} %plan_ref.1), kind=kLoop, calls=%fused_computation | loop fusion | flops 196352 | bytes 3072 | tf_op jit(solution)/shard_map/reduce_sum | solution.py:455
  1.5 67.7 %shard_map.110 = (bf16[1024,32,128]{2,1,0:T(8,128)(2,1)S(1)}, bf16[64,512]{1,0:T(8,128)(2,1)S(1)}, f32[2,64]{1,0:T(2,128)S(1)}, bf16[64,512]{1,0:T(8,128)(2,1)S(1)}, f32[2,64]{1,0:T(2,128)S(1)}) custom-call(s32[256]{0:T(256)} %plan_ref.1, bf16[1,256,8192]{2,1,0:T(8,128)(2,1)} %grad_hbm.1, bf16[256,512]{1,0:T(8,128)(2,1)} %proj_ref.1, ...), custom_call_target="tpu_custom_call" | custom-call | tf_op jit(solution)/shard_map/pallas_call | solution.py:464
  69.2 0.0 copy-done
  69.2 5.0 %shard_map.111 = (bf16[256,8192]{1,0:T(8,128)(2,1)}, bf16[64,512]{1,0:T(8,128)(2,1)}, f32[2,64]{1,0:T(2,128)}, bf16[64,512]{1,0:T(8,128)(2,1)}, f32[2,64]{1,0:T(2,128)}) custom-call(s32[256]{0:T(256)S(1)} %select_reduce_fusion.table_ref, bf16[1024,32,128]{2,1,0:T(8,128)(2,1)S(1)} %get-tuple-element.15.whole, bf16[256,512]{1,0:T(8,128)(2,1)S(1)} %copy-done, ...), custom_call_target="tpu_custom_call" | custom-call | tf_op jit(solution)/shard_map/pallas_call | solution.py:501
  (1 shorter events, 0.0 us)
Async XLA Ops:
  0.6 68.6 %copy-start = (bf16[256,512]{1,0:T(8,128)(2,1)S(1)}, bf16[256,512]{1,0:T(8,128)(2,1)}, u32[]{:S(2)}) copy-start(bf16[256,512]{1,0:T(8,128)(2,1)} %proj_ref.1) | copy-start | bytes 786436
